TPU v7x, 512 devices: a whole 4x8x8 slice. The times are simulated.
512 devices in a mesh: section: 32 (over x, z), replica: 16 (over y, core).
Axes of the slice: x: 4, y: 8, z: 8, core: 2. Of those that a mesh axis runs over, the one named last changes fastest.
Arguments:
- hidden_in: bfloat16 [128, 8192], P('replica'), may hold values from -6 to 6
- norm_gain: float32 [32, 8192], P('section'), may hold values from 0.5 to 2
- new_kv: bfloat16 [32, 128, 2, 4, 128], P('section', 'replica'), may hold values from -6 to 6
- parked: bfloat16 [32, 256, 2, 4, 128, 128], P('section', 'replica'), may hold values from -6 to 6
- cache_len: int32 [128], P('replica'), may hold values from 1 to 256
- block_home: int32 [128, 2], P('replica'), may hold values from 0 to 255, as said below
Outputs:
- section_outputs: bfloat16 [32, 128, 8192], P('section', 'replica')
Inputs may be any that keep to these rules, and one draw needn't show every extreme that they name: `block_home`: every parked block is named exactly once. Parked block b lies on replica b // 16. The rows of replica r name exactly 2 blocks lying on each of replicas r + 8, r + 16 // 2 + 1, ..., r + 16 - 1 (counted cyclically) and none on the others.
All inputs are finite; a program needn't handle non-finite values.
Results may differ from a plain program's by a relative error of at most 0.035.
Values may be sent and summed in bfloat16 or wider, within the bound.
A program may use at most 64 MiB of HBM per device.

v0:
```python
import jax
import jax.numpy as jnp
from jax import lax
from jax.sharding import PartitionSpec as P

HQ = 64
KVH = 4
HD = 128
BLK = 128
NB = 2
MICRO = 4


def from_behind(value, axis, steps):
    count = lax.axis_size(axis)
    first, last = (max(0, -steps), min(count, count - steps))
    return lax.ppermute(value, axis, [(source, source + steps) for source in range(first, last)])


def layer_rows(x, gain, cache, new_kv, lens):
    rows = x.shape[0]
    group = HQ // KVH
    xf = x.astype(jnp.float32)
    normed = xf * lax.rsqrt(jnp.mean(xf * xf, axis=-1, keepdims=True) + 1e-05) * gain
    q = normed.astype(jnp.bfloat16).reshape(rows, KVH, group, HD)
    keys = cache[:, :, 0]
    vals = cache[:, :, 1]
    scale = 1.0 / HD**0.5
    scores = jnp.einsum("rkgd,rnktd->rkgnt", q, keys, preferred_element_type=jnp.float32) * scale
    pos = jnp.arange(NB * BLK, dtype=jnp.int32).reshape(NB, BLK)
    valid = pos[None, :, :] < lens[:, None, None]
    scores = jnp.where(valid[:, None, None, :, :], scores, -1e30)
    new_score = (
        jnp.einsum("rkgd,rkd->rkg", q, new_kv[:, 0], preferred_element_type=jnp.float32) * scale
    )
    top = jnp.maximum(jnp.max(scores, axis=(3, 4)), new_score)
    expo = jnp.exp(scores - top[..., None, None])
    expo_new = jnp.exp(new_score - top)
    total = jnp.sum(expo, axis=(3, 4)) + expo_new
    weights = (expo / total[..., None, None]).astype(jnp.bfloat16)
    weight_new = (expo_new / total).astype(jnp.bfloat16).astype(jnp.float32)
    attended = jnp.einsum("rkgnt,rnktd->rkgd", weights, vals, preferred_element_type=jnp.float32)
    attended = attended + weight_new[..., None] * new_kv[:, 1].astype(jnp.float32)[:, :, None, :]
    return (xf + attended.reshape(rows, HQ * HD)).astype(jnp.bfloat16)


def pick_ranked(sources, local_ids, target, slots):
    matched = sources == target
    ranked = jnp.cumsum(matched.astype(jnp.int32), axis=-1) - 1
    wanted = jnp.arange(slots, dtype=jnp.int32)
    hits = matched[..., None] & (ranked[..., None] == wanted)
    chosen = jnp.sum(jnp.where(hits, local_ids[..., None], 0), axis=-2)
    return (chosen, jnp.any(hits, axis=-2).astype(jnp.int32))


def per_device(hidden_in, norm_gain, new_kv, parked, cache_len, block_home):
    replicas = lax.axis_size("replica")
    me_replica = lax.axis_index("replica")
    blocks = parked[0]
    park_count = blocks.shape[0]
    rows = block_home.shape[0]
    count = rows * NB
    slots = 2 * count // replicas
    wanted_flat = block_home.reshape(count)
    wanted_src = wanted_flat // park_count
    everyone = lax.all_gather(block_home, "replica", axis=0, tiled=True).reshape(replicas, count)
    send_ids, send_flags = pick_ranked(
        everyone // park_count, everyone % park_count, me_replica, slots
    )
    position = jnp.arange(count, dtype=jnp.int32)
    earlier = (wanted_src[:, None] == wanted_src[None, :]) & (position[:, None] > position[None, :])
    rank_in = jnp.sum(earlier.astype(jnp.int32), axis=1)
    outgoing = jnp.take(blocks, send_ids.reshape(-1), axis=0)
    outgoing = outgoing.reshape((replicas, slots) + blocks.shape[1:])
    outgoing = jnp.where(
        send_flags[:, :, None, None, None, None] > 0, outgoing, jnp.zeros((), jnp.bfloat16)
    )
    incoming = lax.all_to_all(outgoing, "replica", split_axis=0, concat_axis=0, tiled=True)
    slot_index = wanted_src * slots + rank_in
    cache = jnp.take(incoming.reshape((replicas * slots,) + blocks.shape[1:]), slot_index, axis=0)
    cache = cache.reshape((rows, NB) + blocks.shape[1:])
    groups = MICRO
    group_rows = rows // groups
    sections = lax.axis_size("section")
    me_section = lax.axis_index("section")
    gain = norm_gain[0]
    kv_new = new_kv[0]
    width = hidden_in.shape[1]

    def step(turn, carry):
        inbox, outbuf = carry
        which = turn - me_section
        active = (which >= 0) & (which < groups)
        start = jnp.clip(which, 0, groups - 1) * group_rows
        first_rows = lax.dynamic_slice_in_dim(hidden_in, start, group_rows, 0)
        source_rows = jnp.where(me_section == 0, first_rows, inbox)
        result = layer_rows(
            source_rows,
            gain,
            lax.dynamic_slice_in_dim(cache, start, group_rows, 0),
            lax.dynamic_slice_in_dim(kv_new, start, group_rows, 0),
            lax.dynamic_slice_in_dim(cache_len, start, group_rows, 0),
        )
        updated = lax.dynamic_update_slice_in_dim(outbuf, result, start, 0)
        outbuf = jnp.where(active, updated, outbuf)
        inbox = from_behind(result, "section", 1)
        return (inbox, outbuf)

    inbox0 = jnp.zeros((group_rows, width), jnp.bfloat16)
    outbuf0 = jnp.zeros((rows, width), jnp.bfloat16)
    final_inbox, outbuf = lax.fori_loop(0, sections + groups - 1, step, (inbox0, outbuf0))
    return outbuf[None]


def solution(mesh):
    return jax.shard_map(
        per_device,
        mesh=mesh,
        in_specs=(
            P("replica", None),
            P("section", None),
            P("section", "replica", None, None, None),
            P("section", "replica", None, None, None, None),
            P("replica"),
            P("replica", None),
        ),
        out_specs=P("section", "replica", None),
        check_vma=False,
    )
```

profile of v0, /device:TPU:6, one launch (start us, length us, event | category | flops | bytes accessed | tf_op | source)
XLA Modules:
  0.0 648.5 jit_solution(13060387063400538834)
XLA Ops:
  0.0 17.8 %all-gather = s32[16,8,2]{1,2,0:T(2,128)S(1)} all-gather(s32[1,8,2]{1,2,0:T(2,128)} %bitcast.96), channel_id=1, replica_groups=mesh['section'=32,'replica'=16] {'replica'}, dimensions={0}, use_global_device_ids=true | all-gather | bytes 1088 | tf_op jit(solution)/shard_map/all_gather | solution.py:66
  18.8 7.2 %gather_fusion = bf16[32,2,4,128,128]{4,3,2,1,0:T(8,128)(2,1)} fusion(bf16[16,2,4,128,128]{4,3,2,1,0:T(8,128)(2,1)} %bitcast.86, s32[1024]{0:T(1024)S(1)} %pad_clamp_fusion.1), kind=kCustom, calls=%fused_computation | custom fusion | bytes 16777344 | tf_op jit(solution)/shard_map/jit(_take)/gather | solution.py:73
  26.0 7.6 %select_select_fusion = bf16[16,2,2,4,128,128]{5,4,3,2,1,0:T(8,128)(2,1)} fusion(bf16[16,2,2,4,128,128]{5,4,3,2,1,0:T(8,128)(2,1)} %bitcast.85, pred[16,2]{1,0:T(8,128)(4,1)S(1)} %copy.52, pred[16,2]{1,0:T(8,128)(4,1)S(1)} %copy.51), kind=kLoop, calls=%fused_computation.40 | loop fusion | flops 8388608 | bytes 16777280 | tf_op jit(solution)/shard_map/jit(_where)/select_n | solution.py:75
  33.6 4.9 all-to-all-start
  39.1 183.5 %all-to-all-done = bf16[16,2,2,4,128,128]{5,4,3,2,1,0:T(8,128)(2,1)} async-done(((bf16[16,2,2,4,128,128]{5,4,3,2,1,0:T(8,128)(2,1)}), bf16[16,2,2,4,128,128]{5,4,3,2,1,0:T(8,128)(2,1)}, u32[]{:S(2)}, u32[]{:S(2)}) %all-to-all-start) | async-done | bytes 8388640 | tf_op jit(solution)/shard_map/all_to_all | solution.py:78
  222.6 6.4 gather_fusion.1
  229.1 4.6 broadcast_select_fusion.2
  233.7 414.1 %while.16 = (s32[]{:T(128)}, bf16[2,8192]{1,0:T(2,128)(2,1)S(1)}, bf16[8,8192]{1,0:T(8,128)(2,1)S(1)}, pred[]{:T(512)}, s32[]{:T(128)}, /*index=5*/bf16[8,8192]{...) while((s32[]{:T(128)}, bf16[2,8192]{1,0:T(2,128)(2,1)S(1)}, ...), condition=%wide.region_8.9_spmd, body=%wide.region_4.8_spmd.sunk | while | flops 17304464 | bytes 4287374 | solution.py:111
  237.5 4.3 collective-permute-start
  241.8 8.8 %collective-permute-done = bf16[2,8192]{1,0:T(2,128)(2,1)S(1)} collective-permute-done((bf16[2,8192]{1,0:T(2,128)(2,1)S(1)}, bf16[2,8192]{1,0:T(2,128)(2,1)S(1)}, u32[]{:S(2)}, u32[]{:S(2)}) %collective-permute-start) | collective-permute-done | bytes 32800 | tf_op jit(solution)/shard_map/while/body/eval_jaxpr/ppermute | solution.py:17
  254.4 1.9 collective-permute-start
  256.3 6.0 collective-permute-done
  266.1 1.9 collective-permute-start
  268.0 6.0 collective-permute-done
  277.7 1.9 collective-permute-start
  279.7 6.0 collective-permute-done
  289.4 1.9 collective-permute-start
  291.4 6.0 collective-permute-done
  301.1 1.9 collective-permute-start
  303.0 6.0 collective-permute-done
  312.8 1.9 collective-permute-start
  314.7 6.0 collective-permute-done
  324.5 1.9 collective-permute-start
  326.4 6.0 collective-permute-done
  336.1 1.9 collective-permute-start
  338.1 6.1 collective-permute-done
  347.9 1.9 collective-permute-start
  349.8 6.0 collective-permute-done
  359.6 1.9 collective-permute-start
  361.5 6.0 collective-permute-done
  371.3 1.9 collective-permute-start
  373.2 6.0 collective-permute-done
  382.9 1.9 collective-permute-start
  384.9 6.0 collective-permute-done
  394.6 1.9 collective-permute-start
  396.6 6.0 collective-permute-done
  406.3 1.9 collective-permute-start
  408.2 6.0 collective-permute-done
  419.9 6.0 collective-permute-done
  429.7 1.9 collective-permute-start
  431.6 6.0 collective-permute-done
  443.3 6.0 collective-permute-done
  455.0 6.0 collective-permute-done
  464.7 1.9 collective-permute-start
  466.6 6.0 collective-permute-done
  478.3 6.0 collective-permute-done
  490.0 6.0 collective-permute-done
  499.7 1.9 collective-permute-start
  501.7 6.0 collective-permute-done
  513.4 6.0 collective-permute-done
  523.1 1.9 collective-permute-start
  525.0 6.0 collective-permute-done
  536.7 6.0 collective-permute-done
  548.4 6.0 collective-permute-done
  558.2 1.9 collective-permute-start
  560.1 6.0 collective-permute-done
  571.8 6.0 collective-permute-done
  583.4 6.0 collective-permute-done
  593.2 1.9 collective-permute-start
  595.1 6.0 collective-permute-done
  606.8 6.0 collective-permute-done
  618.5 6.0 collective-permute-done
  630.2 6.0 collective-permute-done
  641.9 6.0 collective-permute-done
  (611 shorter events, 158.6 us)
Async XLA Ops:
  33.6 4.9 copy-start.3
  33.6 5.4 copy-start.2
  33.6 189.0 %all-to-all-start = ((bf16[16,2,2,4,128,128]{5,4,3,2,1,0:T(8,128)(2,1)}), bf16[16,2,2,4,128,128]{5,4,3,2,1,0:T(8,128)(2,1)}, u32[]{:S(2)}, u32[]{:S(2)}) async-start(bf16[16,2,2,4,128,128]{5,4,3,2,1,0:T(8,128)(2,1)} %select_select_fusion), calls=%async_computation | async-start | bytes 16777216 | tf_op jit(solution)/shard_map/all_to_all | solution.py:78
  229.1 4.6 copy-start
  229.1 4.6 copy-start.4
  237.5 13.1 %collective-permute-start = (bf16[2,8192]{1,0:T(2,128)(2,1)S(1)}, bf16[2,8192]{1,0:T(2,128)(2,1)S(1)}, u32[]{:S(2)}, u32[]{:S(2)}) collective-permute-start(bf16[2,8192]{1,0:T(2,128)(2,1)S(1)} %get-tuple-element.350), channel_id=1, source_target_pairs={{0,16},{16,32},{32,48},{48,64},{64,80},{80,96},{96,112},{112,128},... | collective-permute-start | bytes 98312 | tf_op jit(solution)/shard_map/while/body/eval_jaxpr/ppermute | solution.py:17
  254.4 7.9 %collective-permute-start = (bf16[2,8192]{1,0:T(2,128)(2,1)S(1)}, bf16[2,8192]{1,0:T(2,128)(2,1)S(1)}, u32[]{:S(2)}, u32[]{:S(2)}) collective-permute-start(bf16[2,8192]{1,0:T(2,128)(2,1)S(1)} %get-tuple-element.350), channel_id=1, source_target_pairs={{0,16},{16,32},{32,48},{48,64},{64,80},{80,96},{96,112},{112,128},... | collective-permute-start | bytes 98312 | tf_op jit(solution)/shard_map/while/body/eval_jaxpr/ppermute | solution.py:17
  266.1 7.9 %collective-permute-start = (bf16[2,8192]{1,0:T(2,128)(2,1)S(1)}, bf16[2,8192]{1,0:T(2,128)(2,1)S(1)}, u32[]{:S(2)}, u32[]{:S(2)}) collective-permute-start(bf16[2,8192]{1,0:T(2,128)(2,1)S(1)} %get-tuple-element.350), channel_id=1, source_target_pairs={{0,16},{16,32},{32,48},{48,64},{64,80},{80,96},{96,112},{112,128},... | collective-permute-start | bytes 98312 | tf_op jit(solution)/shard_map/while/body/eval_jaxpr/ppermute | solution.py:17
  277.7 7.9 %collective-permute-start = (bf16[2,8192]{1,0:T(2,128)(2,1)S(1)}, bf16[2,8192]{1,0:T(2,128)(2,1)S(1)}, u32[]{:S(2)}, u32[]{:S(2)}) collective-permute-start(bf16[2,8192]{1,0:T(2,128)(2,1)S(1)} %get-tuple-element.350), channel_id=1, source_target_pairs={{0,16},{16,32},{32,48},{48,64},{64,80},{80,96},{96,112},{112,128},... | collective-permute-start | bytes 98312 | tf_op jit(solution)/shard_map/while/body/eval_jaxpr/ppermute | solution.py:17
  289.4 7.9 %collective-permute-start = (bf16[2,8192]{1,0:T(2,128)(2,1)S(1)}, bf16[2,8192]{1,0:T(2,128)(2,1)S(1)}, u32[]{:S(2)}, u32[]{:S(2)}) collective-permute-start(bf16[2,8192]{1,0:T(2,128)(2,1)S(1)} %get-tuple-element.350), channel_id=1, source_target_pairs={{0,16},{16,32},{32,48},{48,64},{64,80},{80,96},{96,112},{112,128},... | collective-permute-start | bytes 98312 | tf_op jit(solution)/shard_map/while/body/eval_jaxpr/ppermute | solution.py:17
  301.1 7.9 %collective-permute-start = (bf16[2,8192]{1,0:T(2,128)(2,1)S(1)}, bf16[2,8192]{1,0:T(2,128)(2,1)S(1)}, u32[]{:S(2)}, u32[]{:S(2)}) collective-permute-start(bf16[2,8192]{1,0:T(2,128)(2,1)S(1)} %get-tuple-element.350), channel_id=1, source_target_pairs={{0,16},{16,32},{32,48},{48,64},{64,80},{80,96},{96,112},{112,128},... | collective-permute-start | bytes 98312 | tf_op jit(solution)/shard_map/while/body/eval_jaxpr/ppermute | solution.py:17
  312.8 7.9 %collective-permute-start = (bf16[2,8192]{1,0:T(2,128)(2,1)S(1)}, bf16[2,8192]{1,0:T(2,128)(2,1)S(1)}, u32[]{:S(2)}, u32[]{:S(2)}) collective-permute-start(bf16[2,8192]{1,0:T(2,128)(2,1)S(1)} %get-tuple-element.350), channel_id=1, source_target_pairs={{0,16},{16,32},{32,48},{48,64},{64,80},{80,96},{96,112},{112,128},... | collective-permute-start | bytes 98312 | tf_op jit(solution)/shard_map/while/body/eval_jaxpr/ppermute | solution.py:17
  324.5 7.9 %collective-permute-start = (bf16[2,8192]{1,0:T(2,128)(2,1)S(1)}, bf16[2,8192]{1,0:T(2,128)(2,1)S(1)}, u32[]{:S(2)}, u32[]{:S(2)}) collective-permute-start(bf16[2,8192]{1,0:T(2,128)(2,1)S(1)} %get-tuple-element.350), channel_id=1, source_target_pairs={{0,16},{16,32},{32,48},{48,64},{64,80},{80,96},{96,112},{112,128},... | collective-permute-start | bytes 98312 | tf_op jit(solution)/shard_map/while/body/eval_jaxpr/ppermute | solution.py:17
  336.1 8.0 %collective-permute-start = (bf16[2,8192]{1,0:T(2,128)(2,1)S(1)}, bf16[2,8192]{1,0:T(2,128)(2,1)S(1)}, u32[]{:S(2)}, u32[]{:S(2)}) collective-permute-start(bf16[2,8192]{1,0:T(2,128)(2,1)S(1)} %get-tuple-element.350), channel_id=1, source_target_pairs={{0,16},{16,32},{32,48},{48,64},{64,80},{80,96},{96,112},{112,128},... | collective-permute-start | bytes 98312 | tf_op jit(solution)/shard_map/while/body/eval_jaxpr/ppermute | solution.py:17
  347.9 7.9 %collective-permute-start = (bf16[2,8192]{1,0:T(2,128)(2,1)S(1)}, bf16[2,8192]{1,0:T(2,128)(2,1)S(1)}, u32[]{:S(2)}, u32[]{:S(2)}) collective-permute-start(bf16[2,8192]{1,0:T(2,128)(2,1)S(1)} %get-tuple-element.350), channel_id=1, source_target_pairs={{0,16},{16,32},{32,48},{48,64},{64,80},{80,96},{96,112},{112,128},... | collective-permute-start | bytes 98312 | tf_op jit(solution)/shard_map/while/body/eval_jaxpr/ppermute | solution.py:17
  359.6 7.9 %collective-permute-start = (bf16[2,8192]{1,0:T(2,128)(2,1)S(1)}, bf16[2,8192]{1,0:T(2,128)(2,1)S(1)}, u32[]{:S(2)}, u32[]{:S(2)}) collective-permute-start(bf16[2,8192]{1,0:T(2,128)(2,1)S(1)} %get-tuple-element.350), channel_id=1, source_target_pairs={{0,16},{16,32},{32,48},{48,64},{64,80},{80,96},{96,112},{112,128},... | collective-permute-start | bytes 98312 | tf_op jit(solution)/shard_map/while/body/eval_jaxpr/ppermute | solution.py:17
  371.3 7.9 %collective-permute-start = (bf16[2,8192]{1,0:T(2,128)(2,1)S(1)}, bf16[2,8192]{1,0:T(2,128)(2,1)S(1)}, u32[]{:S(2)}, u32[]{:S(2)}) collective-permute-start(bf16[2,8192]{1,0:T(2,128)(2,1)S(1)} %get-tuple-element.350), channel_id=1, source_target_pairs={{0,16},{16,32},{32,48},{48,64},{64,80},{80,96},{96,112},{112,128},... | collective-permute-start | bytes 98312 | tf_op jit(solution)/shard_map/while/body/eval_jaxpr/ppermute | solution.py:17
  382.9 7.9 %collective-permute-start = (bf16[2,8192]{1,0:T(2,128)(2,1)S(1)}, bf16[2,8192]{1,0:T(2,128)(2,1)S(1)}, u32[]{:S(2)}, u32[]{:S(2)}) collective-permute-start(bf16[2,8192]{1,0:T(2,128)(2,1)S(1)} %get-tuple-element.350), channel_id=1, source_target_pairs={{0,16},{16,32},{32,48},{48,64},{64,80},{80,96},{96,112},{112,128},... | collective-permute-start | bytes 98312 | tf_op jit(solution)/shard_map/while/body/eval_jaxpr/ppermute | solution.py:17
  394.6 7.9 %collective-permute-start = (bf16[2,8192]{1,0:T(2,128)(2,1)S(1)}, bf16[2,8192]{1,0:T(2,128)(2,1)S(1)}, u32[]{:S(2)}, u32[]{:S(2)}) collective-permute-start(bf16[2,8192]{1,0:T(2,128)(2,1)S(1)} %get-tuple-element.350), channel_id=1, source_target_pairs={{0,16},{16,32},{32,48},{48,64},{64,80},{80,96},{96,112},{112,128},... | collective-permute-start | bytes 98312 | tf_op jit(solution)/shard_map/while/body/eval_jaxpr/ppermute | solution.py:17
  406.3 7.9 %collective-permute-start = (bf16[2,8192]{1,0:T(2,128)(2,1)S(1)}, bf16[2,8192]{1,0:T(2,128)(2,1)S(1)}, u32[]{:S(2)}, u32[]{:S(2)}) collective-permute-start(bf16[2,8192]{1,0:T(2,128)(2,1)S(1)} %get-tuple-element.350), channel_id=1, source_target_pairs={{0,16},{16,32},{32,48},{48,64},{64,80},{80,96},{96,112},{112,128},... | collective-permute-start | bytes 98312 | tf_op jit(solution)/shard_map/while/body/eval_jaxpr/ppermute | solution.py:17
  418.0 7.9 %collective-permute-start = (bf16[2,8192]{1,0:T(2,128)(2,1)S(1)}, bf16[2,8192]{1,0:T(2,128)(2,1)S(1)}, u32[]{:S(2)}, u32[]{:S(2)}) collective-permute-start(bf16[2,8192]{1,0:T(2,128)(2,1)S(1)} %get-tuple-element.350), channel_id=1, source_target_pairs={{0,16},{16,32},{32,48},{48,64},{64,80},{80,96},{96,112},{112,128},... | collective-permute-start | bytes 98312 | tf_op jit(solution)/shard_map/while/body/eval_jaxpr/ppermute | solution.py:17
  429.7 7.9 %collective-permute-start = (bf16[2,8192]{1,0:T(2,128)(2,1)S(1)}, bf16[2,8192]{1,0:T(2,128)(2,1)S(1)}, u32[]{:S(2)}, u32[]{:S(2)}) collective-permute-start(bf16[2,8192]{1,0:T(2,128)(2,1)S(1)} %get-tuple-element.350), channel_id=1, source_target_pairs={{0,16},{16,32},{32,48},{48,64},{64,80},{80,96},{96,112},{112,128},... | collective-permute-start | bytes 98312 | tf_op jit(solution)/shard_map/while/body/eval_jaxpr/ppermute | solution.py:17
  441.3 7.9 %collective-permute-start = (bf16[2,8192]{1,0:T(2,128)(2,1)S(1)}, bf16[2,8192]{1,0:T(2,128)(2,1)S(1)}, u32[]{:S(2)}, u32[]{:S(2)}) collective-permute-start(bf16[2,8192]{1,0:T(2,128)(2,1)S(1)} %get-tuple-element.350), channel_id=1, source_target_pairs={{0,16},{16,32},{32,48},{48,64},{64,80},{80,96},{96,112},{112,128},... | collective-permute-start | bytes 98312 | tf_op jit(solution)/shard_map/while/body/eval_jaxpr/ppermute | solution.py:17
  453.0 7.9 %collective-permute-start = (bf16[2,8192]{1,0:T(2,128)(2,1)S(1)}, bf16[2,8192]{1,0:T(2,128)(2,1)S(1)}, u32[]{:S(2)}, u32[]{:S(2)}) collective-permute-start(bf16[2,8192]{1,0:T(2,128)(2,1)S(1)} %get-tuple-element.350), channel_id=1, source_target_pairs={{0,16},{16,32},{32,48},{48,64},{64,80},{80,96},{96,112},{112,128},... | collective-permute-start | bytes 98312 | tf_op jit(solution)/shard_map/while/body/eval_jaxpr/ppermute | solution.py:17
  464.7 7.9 %collective-permute-start = (bf16[2,8192]{1,0:T(2,128)(2,1)S(1)}, bf16[2,8192]{1,0:T(2,128)(2,1)S(1)}, u32[]{:S(2)}, u32[]{:S(2)}) collective-permute-start(bf16[2,8192]{1,0:T(2,128)(2,1)S(1)} %get-tuple-element.350), channel_id=1, source_target_pairs={{0,16},{16,32},{32,48},{48,64},{64,80},{80,96},{96,112},{112,128},... | collective-permute-start | bytes 98312 | tf_op jit(solution)/shard_map/while/body/eval_jaxpr/ppermute | solution.py:17
  476.4 7.9 %collective-permute-start = (bf16[2,8192]{1,0:T(2,128)(2,1)S(1)}, bf16[2,8192]{1,0:T(2,128)(2,1)S(1)}, u32[]{:S(2)}, u32[]{:S(2)}) collective-permute-start(bf16[2,8192]{1,0:T(2,128)(2,1)S(1)} %get-tuple-element.350), channel_id=1, source_target_pairs={{0,16},{16,32},{32,48},{48,64},{64,80},{80,96},{96,112},{112,128},... | collective-permute-start | bytes 98312 | tf_op jit(solution)/shard_map/while/body/eval_jaxpr/ppermute | solution.py:17
  488.1 7.9 %collective-permute-start = (bf16[2,8192]{1,0:T(2,128)(2,1)S(1)}, bf16[2,8192]{1,0:T(2,128)(2,1)S(1)}, u32[]{:S(2)}, u32[]{:S(2)}) collective-permute-start(bf16[2,8192]{1,0:T(2,128)(2,1)S(1)} %get-tuple-element.350), channel_id=1, source_target_pairs={{0,16},{16,32},{32,48},{48,64},{64,80},{80,96},{96,112},{112,128},... | collective-permute-start | bytes 98312 | tf_op jit(solution)/shard_map/while/body/eval_jaxpr/ppermute | solution.py:17
  499.7 7.9 %collective-permute-start = (bf16[2,8192]{1,0:T(2,128)(2,1)S(1)}, bf16[2,8192]{1,0:T(2,128)(2,1)S(1)}, u32[]{:S(2)}, u32[]{:S(2)}) collective-permute-start(bf16[2,8192]{1,0:T(2,128)(2,1)S(1)} %get-tuple-element.350), channel_id=1, source_target_pairs={{0,16},{16,32},{32,48},{48,64},{64,80},{80,96},{96,112},{112,128},... | collective-permute-start | bytes 98312 | tf_op jit(solution)/shard_map/while/body/eval_jaxpr/ppermute | solution.py:17
  511.4 7.9 %collective-permute-start = (bf16[2,8192]{1,0:T(2,128)(2,1)S(1)}, bf16[2,8192]{1,0:T(2,128)(2,1)S(1)}, u32[]{:S(2)}, u32[]{:S(2)}) collective-permute-start(bf16[2,8192]{1,0:T(2,128)(2,1)S(1)} %get-tuple-element.350), channel_id=1, source_target_pairs={{0,16},{16,32},{32,48},{48,64},{64,80},{80,96},{96,112},{112,128},... | collective-permute-start | bytes 98312 | tf_op jit(solution)/shard_map/while/body/eval_jaxpr/ppermute | solution.py:17
  523.1 7.9 %collective-permute-start = (bf16[2,8192]{1,0:T(2,128)(2,1)S(1)}, bf16[2,8192]{1,0:T(2,128)(2,1)S(1)}, u32[]{:S(2)}, u32[]{:S(2)}) collective-permute-start(bf16[2,8192]{1,0:T(2,128)(2,1)S(1)} %get-tuple-element.350), channel_id=1, source_target_pairs={{0,16},{16,32},{32,48},{48,64},{64,80},{80,96},{96,112},{112,128},... | collective-permute-start | bytes 98312 | tf_op jit(solution)/shard_map/while/body/eval_jaxpr/ppermute | solution.py:17
  534.8 7.9 %collective-permute-start = (bf16[2,8192]{1,0:T(2,128)(2,1)S(1)}, bf16[2,8192]{1,0:T(2,128)(2,1)S(1)}, u32[]{:S(2)}, u32[]{:S(2)}) collective-permute-start(bf16[2,8192]{1,0:T(2,128)(2,1)S(1)} %get-tuple-element.350), channel_id=1, source_target_pairs={{0,16},{16,32},{32,48},{48,64},{64,80},{80,96},{96,112},{112,128},... | collective-permute-start | bytes 98312 | tf_op jit(solution)/shard_map/while/body/eval_jaxpr/ppermute | solution.py:17
  546.5 7.9 %collective-permute-start = (bf16[2,8192]{1,0:T(2,128)(2,1)S(1)}, bf16[2,8192]{1,0:T(2,128)(2,1)S(1)}, u32[]{:S(2)}, u32[]{:S(2)}) collective-permute-start(bf16[2,8192]{1,0:T(2,128)(2,1)S(1)} %get-tuple-element.350), channel_id=1, source_target_pairs={{0,16},{16,32},{32,48},{48,64},{64,80},{80,96},{96,112},{112,128},... | collective-permute-start | bytes 98312 | tf_op jit(solution)/shard_map/while/body/eval_jaxpr/ppermute | solution.py:17
  558.2 7.9 %collective-permute-start = (bf16[2,8192]{1,0:T(2,128)(2,1)S(1)}, bf16[2,8192]{1,0:T(2,128)(2,1)S(1)}, u32[]{:S(2)}, u32[]{:S(2)}) collective-permute-start(bf16[2,8192]{1,0:T(2,128)(2,1)S(1)} %get-tuple-element.350), channel_id=1, source_target_pairs={{0,16},{16,32},{32,48},{48,64},{64,80},{80,96},{96,112},{112,128},... | collective-permute-start | bytes 98312 | tf_op jit(solution)/shard_map/while/body/eval_jaxpr/ppermute | solution.py:17
  569.8 7.9 %collective-permute-start = (bf16[2,8192]{1,0:T(2,128)(2,1)S(1)}, bf16[2,8192]{1,0:T(2,128)(2,1)S(1)}, u32[]{:S(2)}, u32[]{:S(2)}) collective-permute-start(bf16[2,8192]{1,0:T(2,128)(2,1)S(1)} %get-tuple-element.350), channel_id=1, source_target_pairs={{0,16},{16,32},{32,48},{48,64},{64,80},{80,96},{96,112},{112,128},... | collective-permute-start | bytes 98312 | tf_op jit(solution)/shard_map/while/body/eval_jaxpr/ppermute | solution.py:17
  581.5 7.9 %collective-permute-start = (bf16[2,8192]{1,0:T(2,128)(2,1)S(1)}, bf16[2,8192]{1,0:T(2,128)(2,1)S(1)}, u32[]{:S(2)}, u32[]{:S(2)}) collective-permute-start(bf16[2,8192]{1,0:T(2,128)(2,1)S(1)} %get-tuple-element.350), channel_id=1, source_target_pairs={{0,16},{16,32},{32,48},{48,64},{64,80},{80,96},{96,112},{112,128},... | collective-permute-start | bytes 98312 | tf_op jit(solution)/shard_map/while/body/eval_jaxpr/ppermute | solution.py:17
  593.2 7.9 %collective-permute-start = (bf16[2,8192]{1,0:T(2,128)(2,1)S(1)}, bf16[2,8192]{1,0:T(2,128)(2,1)S(1)}, u32[]{:S(2)}, u32[]{:S(2)}) collective-permute-start(bf16[2,8192]{1,0:T(2,128)(2,1)S(1)} %get-tuple-element.350), channel_id=1, source_target_pairs={{0,16},{16,32},{32,48},{48,64},{64,80},{80,96},{96,112},{112,128},... | collective-permute-start | bytes 98312 | tf_op jit(solution)/shard_map/while/body/eval_jaxpr/ppermute | solution.py:17
  604.9 7.9 %collective-permute-start = (bf16[2,8192]{1,0:T(2,128)(2,1)S(1)}, bf16[2,8192]{1,0:T(2,128)(2,1)S(1)}, u32[]{:S(2)}, u32[]{:S(2)}) collective-permute-start(bf16[2,8192]{1,0:T(2,128)(2,1)S(1)} %get-tuple-element.350), channel_id=1, source_target_pairs={{0,16},{16,32},{32,48},{48,64},{64,80},{80,96},{96,112},{112,128},... | collective-permute-start | bytes 98312 | tf_op jit(solution)/shard_map/while/body/eval_jaxpr/ppermute | solution.py:17
  616.6 7.9 %collective-permute-start = (bf16[2,8192]{1,0:T(2,128)(2,1)S(1)}, bf16[2,8192]{1,0:T(2,128)(2,1)S(1)}, u32[]{:S(2)}, u32[]{:S(2)}) collective-permute-start(bf16[2,8192]{1,0:T(2,128)(2,1)S(1)} %get-tuple-element.350), channel_id=1, source_target_pairs={{0,16},{16,32},{32,48},{48,64},{64,80},{80,96},{96,112},{112,128},... | collective-permute-start | bytes 98312 | tf_op jit(solution)/shard_map/while/body/eval_jaxpr/ppermute | solution.py:17
  628.2 7.9 %collective-permute-start = (bf16[2,8192]{1,0:T(2,128)(2,1)S(1)}, bf16[2,8192]{1,0:T(2,128)(2,1)S(1)}, u32[]{:S(2)}, u32[]{:S(2)}) collective-permute-start(bf16[2,8192]{1,0:T(2,128)(2,1)S(1)} %get-tuple-element.350), channel_id=1, source_target_pairs={{0,16},{16,32},{32,48},{48,64},{64,80},{80,96},{96,112},{112,128},... | collective-permute-start | bytes 98312 | tf_op jit(solution)/shard_map/while/body/eval_jaxpr/ppermute | solution.py:17
  639.9 7.9 %collective-permute-start = (bf16[2,8192]{1,0:T(2,128)(2,1)S(1)}, bf16[2,8192]{1,0:T(2,128)(2,1)S(1)}, u32[]{:S(2)}, u32[]{:S(2)}) collective-permute-start(bf16[2,8192]{1,0:T(2,128)(2,1)S(1)} %get-tuple-element.350), channel_id=1, source_target_pairs={{0,16},{16,32},{32,48},{48,64},{64,80},{80,96},{96,112},{112,128},... | collective-permute-start | bytes 98312 | tf_op jit(solution)/shard_map/while/body/eval_jaxpr/ppermute | solution.py:17
  647.8 0.7 copy-start.1
where the time goes:
time: 651 us; the launch traced here: 648 us
  waiting for transfers between devices  396 us (61%)
  starting transfers between devices  74.4 us (11%)
  other arithmetic  70.1 us (11%)
  local copies, waits for them, and re-layouts  62.6 us (10%)
  matrix products  24.8 us (4%)
  blocking collectives  17.8 us (3%)
    ppermute x35, waiting for transfers between devices, from_behind(): lax.ppermute(value, axis, [(source, source + steps) for source in range(f...  212 us
    all_to_all x1, waiting for transfers between devices, per_device(): lax.all_to_all(outgoing, 'replica', split_axis=0, concat_axis=0, tiled=True)  184 us
    ppermute x35, starting transfers between devices, from_behind(): lax.ppermute(value, axis, [(source, source + steps) for source in range(f...  69.6 us
    slice x35, local copies, waits for them, and re-layouts, layer_rows(): keys = cache[:, :, 0]  44.4 us
    reduce_sum x35, other arithmetic, layer_rows(): jnp.mean(xf * xf, axis=-1, keepdims=True) + 1e-05  38.3 us
    all_gather x1, blocking collectives, per_device(): lax.all_gather(block_home, 'replica', axis=0, tiled=True)  17.8 us
  transfers between devices with their start and end apart: 36, of which 36 were waited for; matrix products, arithmetic and copies ran while one was open for 0% of the time, Pallas kernels for 0%

commit v1 on v0

v1 whole, which is shorter than its diff:
```python
import functools
import math

import jax
import jax.numpy as jnp
from jax import lax
from jax.experimental import pallas as pl
from jax.experimental.pallas import tpu as pltpu
from jax.sharding import PartitionSpec as P

HQ = 64
KVH = 4
HD = 128
BLK = 128
NB = 2
GROUP = HQ // KVH
HALF = 8
MID = 4
STEP = 1
MESH = pl.DeviceIdType.MESH


def dot_t(a, b):
    return lax.dot_general(a, b, (((1,), (1,)), ((), ())), preferred_element_type=jnp.float32)


def dot(a, b):
    return jnp.dot(a, b, preferred_element_type=jnp.float32)


def layer_row(x, gain, kv, slots, length, new):
    xf = x.astype(jnp.float32)
    q = (xf * gain).astype(jnp.bfloat16)
    square = jnp.sum(jnp.sum(xf * xf, axis=0, keepdims=True), axis=1, keepdims=True)
    factor = lax.rsqrt(square * (1.0 / (HQ * HD)) + 1e-05) * (math.log2(math.e) / HD**0.5)
    pos = lax.broadcasted_iota(jnp.int32, (1, NB * BLK), 1)
    bias = jnp.where(pos < length, 0.0, -1e30)
    scores = []
    news = []
    for h in range(KVH):
        qh = q[h * GROUP : (h + 1) * GROUP]
        parts = [dot_t(qh, kv[slots[j], 0, h]) for j in range(NB)]
        scores.append(jnp.concatenate(parts, axis=1))
        news.append(
            jnp.sum(qh.astype(jnp.float32) * new[h : h + 1], axis=1, keepdims=True)
        )
    score = jnp.concatenate(scores, axis=0) + bias
    score_new = jnp.concatenate(news, axis=0)
    top = jnp.maximum(jnp.max(score, axis=1, keepdims=True), score_new)
    expo = jnp.exp2((score - top) * factor)
    expo_new = jnp.exp2((score_new - top) * factor)
    total = jnp.sum(expo, axis=1, keepdims=True) + expo_new
    weights = expo.astype(jnp.bfloat16)
    outs = []
    for h in range(KVH):
        rows = slice(h * GROUP, (h + 1) * GROUP)
        part = expo_new[rows] * new[KVH + h : KVH + h + 1]
        for j in range(NB):
            part = part + dot(weights[rows, j * BLK : (j + 1) * BLK], kv[slots[j], 1, h])
        outs.append(part)
    attended = jnp.concatenate(outs, axis=0) / total
    return (xf + attended).astype(jnp.bfloat16)


def kernel(
    sections, replicas, rows,
    meta_ref, hidden_ref, new_ref, gain_ref, parked_ref, out_ref,
    park, send, kv, metav, metas, x_in, x_out, new_in, new_f,
    park_sem, smem_sem, meta_send, meta_recv, kv_send, kv_recv,
    x_send, x_recv, out_send, out_recv, first_send, new_send, new_recv,
):
    s = lax.axis_index("section")
    p = lax.axis_index("replica")
    turns = rows // STEP

    def at(shift):
        return {"replica": lax.rem(p + shift + 2 * replicas, replicas)}

    park_copy = pltpu.make_async_copy(parked_ref, park, park_sem)
    park_copy.start()

    barrier = pltpu.get_barrier_semaphore()

    @pl.loop(1, replicas)
    def _(j):
        pl.semaphore_signal(barrier, inc=1, device_id=at(j), device_id_type=MESH)

    @pl.when(s > 0)
    def _():
        pl.semaphore_signal(barrier, inc=1, device_id={"section": s - 1}, device_id_type=MESH)

    pl.semaphore_wait(barrier, replicas - 1 + (s < sections - 1).astype(jnp.int32))

    def meta_copy(k):
        return pltpu.make_async_remote_copy(
            meta_ref, metav.at[k], meta_send.at[k], meta_recv.at[k],
            device_id=at(HALF + k), device_id_type=MESH,
        )

    def hidden_copy(m):
        return pltpu.make_async_remote_copy(
            hidden_ref.at[pl.ds(m * STEP, STEP)], x_in.at[pl.ds(m * STEP, STEP)],
            first_send.at[m], x_recv.at[m],
            device_id=at(HALF + MID), device_id_type=MESH,
        )

    new_copy = pltpu.make_async_remote_copy(
        new_ref, new_in, new_send, new_recv, device_id=at(HALF + MID), device_id_type=MESH
    )

    @pl.loop(0, HALF)
    def _(k):
        meta_copy(k).start()

    new_copy.start()

    @pl.when(s == 0)
    def _():
        @pl.loop(0, turns)
        def _(m):
            hidden_copy(m).start()

    @pl.loop(0, HALF)
    def _(k):
        meta_copy(k).wait_recv()

    to_smem = pltpu.make_async_copy(metav, metas, smem_sem)
    to_smem.start()
    to_smem.wait()
    park_copy.wait()

    def kv_copy(k):
        return pltpu.make_async_remote_copy(
            send.at[pl.ds(NB * k, NB)], kv.at[pl.ds(NB * k, NB)],
            kv_send.at[k], kv_recv.at[k],
            device_id=at(MID - k), device_id_type=MESH,
        )

    def pick(k, dst):
        for j in range(NB):
            block = metas[k, 0, NB * k + j]
            for half in range(2):
                for h in range(KVH):
                    dst[NB * k + j, half, h] = park[block, half, h]

    @pl.loop(0, HALF - 1)
    def _(t):
        k = t + t // MID
        pick(k, send)
        kv_copy(k).start()

    pick(MID, kv)

    new_copy.wait_recv()
    new_f[...] = new_in[...].astype(jnp.float32).reshape(new_f.shape)
    gain = gain_ref[...]

    @pl.loop(0, HALF - 1)
    def _(t):
        kv_copy(t + t // MID).wait_recv()

    def relay_copy(m):
        return pltpu.make_async_remote_copy(
            x_out.at[pl.ds(m * STEP, STEP)], x_in.at[pl.ds(m * STEP, STEP)],
            x_send.at[m], x_recv.at[m],
            device_id={"section": s + 1}, device_id_type=MESH,
        )

    def home_copy(m):
        return pltpu.make_async_remote_copy(
            x_out.at[pl.ds(m * STEP, STEP)], out_ref.at[pl.ds(m * STEP, STEP)],
            out_send.at[m], out_recv.at[m],
            device_id=at(-HALF - MID), device_id_type=MESH,
        )

    @pl.loop(0, turns)
    def _(m):
        hidden_copy(m).wait_recv()
        for i in range(STEP):
            row = m * STEP + i
            slots = [metas[MID, 1, NB * row + j] for j in range(NB)]
            length = metas[MID, 2, row]
            x_out[row] = layer_row(x_in[row], gain, kv, slots, length, new_f[row])

        @pl.when(s < sections - 1)
        def _():
            relay_copy(m).start()

        home_copy(m).start()

    @pl.loop(0, HALF)
    def _(k):
        meta_copy(k).wait_send()

    @pl.loop(0, HALF - 1)
    def _(t):
        kv_copy(t + t // MID).wait_send()

    new_copy.wait_send()

    @pl.when(s == 0)
    def _():
        @pl.loop(0, turns)
        def _(m):
            hidden_copy(m).wait_send()

    @pl.loop(0, turns)
    def _(m):
        @pl.when(s < sections - 1)
        def _():
            relay_copy(m).wait_send()

        home_copy(m).wait_send()
        home_copy(m).wait_recv()


def per_device(hidden_in, norm_gain, new_kv, parked, cache_len, block_home):
    replicas = lax.axis_size("replica")
    sections = lax.axis_size("section")
    me = lax.axis_index("replica")
    blocks = parked[0]
    park_count = blocks.shape[0]
    rows = block_home.shape[0]
    count = rows * NB

    flat = block_home.reshape(count)
    near = lax.rem(flat - (me + HALF) * park_count + 2 * replicas * park_count, replicas * park_count)
    place = jnp.sum((near[None, :] < near[:, None]).astype(jnp.int32), axis=1)
    hit = place[None, :] == jnp.arange(count, dtype=jnp.int32)[:, None]
    local = jnp.sum(jnp.where(hit, lax.rem(flat, park_count)[None, :], 0), axis=1)
    meta = jnp.stack([
        jnp.pad(local, (0, 128 - count)),
        jnp.pad(place, (0, 128 - count)),
        jnp.pad(cache_len, (0, 128 - rows)),
    ])
    meta = jnp.pad(meta, ((0, 5), (0, 0)))

    turns = rows // STEP
    vmem = pl.BlockSpec(memory_space=pltpu.VMEM)
    hbm = pl.BlockSpec(memory_space=pl.ANY)
    dma = pltpu.SemaphoreType.DMA
    out = pl.pallas_call(
        functools.partial(kernel, sections, replicas, rows),
        out_shape=jax.ShapeDtypeStruct((rows, HQ, HD), jnp.bfloat16),
        in_specs=[vmem, vmem, vmem, vmem, hbm],
        out_specs=hbm,
        scratch_shapes=[
            pltpu.VMEM(blocks.shape, jnp.bfloat16),
            pltpu.VMEM(blocks.shape, jnp.bfloat16),
            pltpu.VMEM(blocks.shape, jnp.bfloat16),
            pltpu.VMEM((HALF, 8, 128), jnp.int32),
            pltpu.SMEM((HALF, 8, 128), jnp.int32),
            pltpu.VMEM((rows, HQ, HD), jnp.bfloat16),
            pltpu.VMEM((rows, HQ, HD), jnp.bfloat16),
            pltpu.VMEM((rows * 2 * KVH, HD), jnp.bfloat16),
            pltpu.VMEM((rows, 2 * KVH, HD), jnp.float32),
            dma, dma,
            dma((HALF,)), dma((HALF,)), dma((HALF,)), dma((HALF,)),
            dma((turns,)), dma((turns,)), dma((turns,)), dma((turns,)), dma((turns,)),
            dma, dma,
        ],
        compiler_params=pltpu.CompilerParams(
            collective_id=0, has_side_effects=True, vmem_limit_bytes=32 * 1024 * 1024
        ),
    )(
        meta,
        hidden_in.reshape(rows, HQ, HD),
        new_kv[0].reshape(rows * 2 * KVH, HD),
        norm_gain.reshape(HQ, HD),
        blocks,
    )
    return out.reshape(1, rows, HQ * HD)


def solution(mesh):
    return jax.shard_map(
        per_device,
        mesh=mesh,
        in_specs=(
            P("replica", None),
            P("section", None),
            P("section", "replica", None, None, None),
            P("section", "replica", None, None, None, None),
            P("replica"),
            P("replica", None),
        ),
        out_specs=P("section", "replica", None),
        check_vma=False,
    )
```

time: 651 us -> 187 us (0.29)
  the two profiles are of different devices: /device:TPU:6 before, /device:TPU:454 now
where the time goes in v1:
time: 187 us
  Pallas kernels  180 us (96%)
  local copies, waits for them, and re-layouts  6.81 us (4%)
    pallas_call x1, Pallas kernels, per_device(): pl.pallas_call(functools.partial(kernel, sections, replicas, rows), out_s...  180 us
    unnamed x8, local copies, waits for them, and re-layouts  5.34 us

profile of v1, /device:TPU:454, one launch (start us, length us, event | category | flops | bytes accessed | tf_op | source)
XLA Modules:
  0.0 186.9 jit_solution(2516563563128512739)
XLA Ops:
  0.0 0.8 copy.9
  0.8 0.1 reshape.53
  0.8 0.2 convert_reduce_fusion
  1.0 0.1 select_reduce_fusion
  1.2 0.7 pad_bitcast_fusion
  1.8 0.9 copy.12
  2.8 0.0 copy-start
  2.8 2.2 %copy-done = bf16[1,16,2,4,128,128]{5,4,3,2,1,0:T(8,128)(2,1)S(1)} copy-done((bf16[1,16,2,4,128,128]{5,4,3,2,1,0:T(8,128)(2,1)S(1)}, bf16[1,16,2,4,128,128]{5,4,3,2,1,0:T(8,128)(2,1)}, u32[]{:S(2)}) %copy-start) | copy-done | bytes 4194328
  5.0 0.0 copy-start.1
  5.0 0.8 copy-done.1
  5.7 0.0 copy-start.2
  5.7 0.7 copy-done.2
  6.4 179.7 %shard_map.64 = bf16[8,64,128]{2,1,0:T(8,128)(2,1)S(1)} custom-call(s32[8,128]{1,0:T(8,128)S(1)} %pad.18.meta_ref, bf16[8,64,128]{2,1,0:T(8,128)(2,1)S(1)} %bitcast.14, bf16[64,128]{1,0:T(8,128)(2,1)S(1)} %bitcast.16, f32[64,128]{1,0:T(8,128)S(1)} %bitcast.15, bf16[16,2,4,128,128]{4,3,2,1,0:T(8,128)(2,1)S(1)} %bitcast.13), custom_call_target="tpu_custom_call" | custom-call | tf_op jit(solution)/shard_map/pallas_call | solution.py:242
  186.2 0.7 reshape.56
  (4 shorter events, 0.0 us)
Async XLA Ops:
  2.8 2.2 %copy-start = (bf16[1,16,2,4,128,128]{5,4,3,2,1,0:T(8,128)(2,1)S(1)}, bf16[1,16,2,4,128,128]{5,4,3,2,1,0:T(8,128)(2,1)}, u32[]{:S(2)}) copy-start(bf16[1,16,2,4,128,128]{5,4,3,2,1,0:T(8,128)(2,1)} %param.9) | copy-start | bytes 12582916
  5.0 0.8 copy-start.1
  5.7 0.7 copy-start.2

commit v2 on v1

v2 whole, which is shorter than its diff:
```python
import functools
import math

import jax
import jax.numpy as jnp
from jax import lax
from jax.experimental import pallas as pl
from jax.experimental.pallas import tpu as pltpu
from jax.sharding import PartitionSpec as P

HQ = 64
KVH = 4
HD = 128
BLK = 128
NB = 2
GROUP = HQ // KVH
HALF = 8
MID = 4
MESH = pl.DeviceIdType.MESH


def dot_t(a, b):
    return lax.dot_general(a, b, (((1,), (1,)), ((), ())), preferred_element_type=jnp.float32)


def dot(a, b):
    return jnp.dot(a, b, preferred_element_type=jnp.float32)


def layer_row(x, gain, kv, slots, length, new):
    xf = x.astype(jnp.float32)
    q = (xf * gain).astype(jnp.bfloat16)
    square = jnp.sum(jnp.sum(xf * xf, axis=0, keepdims=True), axis=1, keepdims=True)
    factor = lax.rsqrt(square * (1.0 / (HQ * HD)) + 1e-05) * (math.log2(math.e) / HD**0.5)
    heads = [slice(h * GROUP, (h + 1) * GROUP) for h in range(KVH)]
    pad = jnp.zeros((BLK - 2 * KVH, HD), jnp.float32)
    new_keys, new_values = [
        jnp.concatenate([new[i], pad], axis=0).astype(jnp.bfloat16) for i in range(2)
    ]
    pos = lax.broadcasted_iota(jnp.int32, (1, BLK), 1)
    own = lax.broadcasted_iota(jnp.int32, (HQ, BLK), 0) // GROUP
    masks = [pos + j * BLK < length for j in range(NB)]
    masks.append(lax.broadcasted_iota(jnp.int32, (HQ, BLK), 1) == own)
    cached = jnp.concatenate(
        [
            dot(q[rows], jnp.concatenate([kv[slots[j], 0, h] for j in range(NB)], axis=1))
            for h, rows in enumerate(heads)
        ],
        axis=0,
    )
    scores = [cached[:, j * BLK : (j + 1) * BLK] for j in range(NB)]
    scores.append(dot_t(q, new_keys))
    scores = [part + jnp.where(mask, 0.0, -1e30) for part, mask in zip(scores, masks)]
    top = jnp.max(functools.reduce(jnp.maximum, scores), axis=1, keepdims=True)
    expos = [jnp.exp2((part - top) * factor) for part in scores]
    total = jnp.sum(sum(expos), axis=1, keepdims=True)
    weights = [part.astype(jnp.bfloat16) for part in expos]
    cached = jnp.concatenate(weights[:NB], axis=1)
    attended = dot(weights[NB], new_values) + jnp.concatenate(
        [
            dot(cached[rows], jnp.concatenate([kv[slots[j], 1, h] for j in range(NB)], axis=0))
            for h, rows in enumerate(heads)
        ],
        axis=0,
    )
    return (xf + attended / total).astype(jnp.bfloat16)


def kernel(
    sections, replicas, rows,
    meta_ref, hidden_ref, new_ref, gain_ref, parked_ref, out_ref,
    park, send, kv, metav, metas, hidden, hidden_f, first, x_in, x_out,
    new_raw, new_own, new_in, gain,
    local_sem, meta_send, meta_recv, kv_send, kv_recv,
    x_send, x_recv, out_send, out_recv, first_send, new_send, new_recv,
):
    s = lax.axis_index("section")
    p = lax.axis_index("replica")
    core = lax.rem(p, 2)
    worker = core == 1
    total = 2 * rows

    def at(shift):
        return {"replica": lax.rem(p + shift + 2 * replicas, replicas)}

    def local(i, src, dst):
        return pltpu.make_async_copy(src, dst, local_sem.at[i])

    fetch = [
        local(0, parked_ref, park),
        local(1, hidden_ref, hidden),
        local(2, new_ref, new_raw),
        local(3, gain_ref, gain),
    ]
    for copy in fetch:
        copy.start()

    barrier = pltpu.get_barrier_semaphore()

    @pl.loop(1, replicas)
    def _(j):
        pl.semaphore_signal(barrier, inc=1, device_id=at(j), device_id_type=MESH)

    @pl.when((s > 0) & worker)
    def _():
        pl.semaphore_signal(barrier, inc=1, device_id={"section": s - 1}, device_id_type=MESH)

    next_one = ((s < sections - 1) & worker).astype(jnp.int32)
    pl.semaphore_wait(barrier, replicas - 1 + next_one)

    def meta_copy(k):
        return pltpu.make_async_remote_copy(
            meta_ref, metav.at[k], meta_send.at[k], meta_recv.at[k],
            device_id=at(HALF + k), device_id_type=MESH,
        )

    mine = at(HALF + MID + 1 - core)

    def first_copy(m):
        return pltpu.make_async_remote_copy(
            first.at[m], x_in.at[core * rows + m], first_send.at[m], x_recv.at[core * rows + m],
            device_id=mine, device_id_type=MESH,
        )

    new_copy = pltpu.make_async_remote_copy(
        new_own, new_in.at[core], new_send, new_recv.at[core],
        device_id=mine, device_id_type=MESH,
    )

    @pl.loop(0, HALF)
    def _(k):
        meta_copy(k).start()

    @pl.loop(0, HALF)
    def _(k):
        meta_copy(k).wait_recv()

    to_smem = local(4, metav, metas)
    to_smem.start()
    to_smem.wait()
    fetch[0].wait()

    def target(k):
        to = p + MID - k + 2 * replicas
        return lax.rem(to - lax.rem(to, 2) + 1, replicas)

    def kv_pieces(k):
        home = lax.rem(p - k + 2 * replicas, 2)
        return (
            send.at[pl.ds(NB * k, NB)],
            kv.at[home, pl.ds(NB * k, NB)],
            kv_send.at[k],
            kv_recv.at[home, k],
        )

    def kv_copy(k):
        return pltpu.make_async_remote_copy(
            *kv_pieces(k), device_id={"replica": target(k)}, device_id_type=MESH
        )

    def kv_stay(k):
        src, dst, _, sem = kv_pieces(k)
        return pltpu.make_async_copy(src, dst, sem)

    @pl.loop(0, HALF)
    def _(k):
        for j in range(NB):
            block = metas[k, 0, NB * k + j]
            for h in range(KVH):
                send[NB * k + j, 0, h] = park[block, 0, h].T
                send[NB * k + j, 1, h] = park[block, 1, h]

        @pl.when(target(k) != p)
        def _():
            kv_copy(k).start()

        @pl.when(target(k) == p)
        def _():
            kv_stay(k).start()

    fetch[1].wait()
    fetch[2].wait()
    fetch[3].wait()

    @pl.loop(0, rows)
    def _(m):
        pair = new_raw[0, m].astype(jnp.float32)
        new_own[m, 0] = jnp.concatenate([pair[0], pair[1]], axis=0)
        new_own[m, 1] = jnp.concatenate([pair[1], pair[0]], axis=0)

    new_copy.start()

    @pl.when(s == 0)
    def _():
        for h in range(HQ):
            hidden_f[:, h, :] = hidden[:, h * HD : (h + 1) * HD].astype(jnp.float32)

        @pl.loop(0, rows)
        def _(m):
            first[m] = hidden_f[m].astype(jnp.bfloat16)
            first_copy(m).start()

    def arrival(home, k):
        return pltpu.make_async_remote_copy(
            send.at[pl.ds(0, NB)], kv.at[home, pl.ds(NB * k, NB)],
            kv_send.at[k], kv_recv.at[home, k],
            device_id={"replica": p}, device_id_type=MESH,
        )

    def row_arrival(i):
        return pltpu.make_async_remote_copy(
            x_out.at[i], x_in.at[i], x_send.at[i], x_recv.at[i],
            device_id={"section": s}, device_id_type=MESH,
        )

    def relay_copy(i):
        return pltpu.make_async_remote_copy(
            x_out.at[i], x_in.at[i], x_send.at[i], x_recv.at[i],
            device_id={"section": s + 1}, device_id_type=MESH,
        )

    def home_copy(i):
        home = i // rows
        return pltpu.make_async_remote_copy(
            x_out.at[i], out_ref.at[i - home * rows], out_send.at[i], out_recv.at[i - home * rows],
            device_id=at(MID - 1 + home), device_id_type=MESH,
        )

    @pl.when(worker)
    def _():
        for home in range(2):
            pltpu.make_async_remote_copy(
                new_own, new_in.at[home], new_send, new_recv.at[home],
                device_id={"replica": p}, device_id_type=MESH,
            ).wait_recv()

            @pl.loop(0, HALF)
            def _(k):
                arrival(home, k).wait_recv()

        @pl.loop(0, total)
        def _(i):
            home = i // rows
            row = i - home * rows
            info = MID + 1 - home
            row_arrival(i).wait_recv()
            slots = [metas[info, 1, j * rows + row] for j in range(NB)]
            length = metas[info, 2, row]
            x_out[i] = layer_row(
                x_in[i], gain[...], kv.at[home], slots, length, new_in[home, row]
            )

            @pl.when(s < sections - 1)
            def _():
                relay_copy(i).start()

            home_copy(i).start()

        @pl.loop(0, total)
        def _(i):
            @pl.when(s < sections - 1)
            def _():
                relay_copy(i).wait_send()

            home_copy(i).wait_send()

    @pl.loop(0, HALF)
    def _(k):
        meta_copy(k).wait_send()

        @pl.when(target(k) != p)
        def _():
            kv_copy(k).wait_send()

    new_copy.wait_send()

    @pl.loop(0, rows)
    def _(m):
        @pl.when(s == 0)
        def _():
            first_copy(m).wait_send()

        pltpu.make_async_remote_copy(
            x_out.at[m], out_ref.at[m], out_send.at[m], out_recv.at[m],
            device_id={"replica": p}, device_id_type=MESH,
        ).wait_recv()


def per_device(hidden_in, norm_gain, new_kv, parked, cache_len, block_home):
    replicas = lax.axis_size("replica")
    sections = lax.axis_size("section")
    me = lax.axis_index("replica")
    blocks = parked[0]
    park_count = blocks.shape[0]
    rows = block_home.shape[0]
    count = rows * NB

    flat = block_home.T.reshape(count)
    near = lax.rem(flat - (me + HALF) * park_count + 2 * replicas * park_count, replicas * park_count)
    place = jnp.sum((near[None, :] < near[:, None]).astype(jnp.int32), axis=1)
    hit = place[None, :] == jnp.arange(count, dtype=jnp.int32)[:, None]
    local = jnp.sum(jnp.where(hit, lax.rem(flat, park_count)[None, :], 0), axis=1)
    meta = jnp.stack([
        jnp.pad(local, (0, 128 - count)),
        jnp.pad(place, (0, 128 - count)),
        jnp.pad(cache_len, (0, 128 - rows)),
    ])
    meta = jnp.pad(meta, ((0, 5), (0, 0)))

    total = 2 * rows
    hbm = pl.BlockSpec(memory_space=pl.ANY)
    dma = pltpu.SemaphoreType.DMA
    out = pl.pallas_call(
        functools.partial(kernel, sections, replicas, rows),
        out_shape=jax.ShapeDtypeStruct((rows, HQ, HD), jnp.bfloat16),
        in_specs=[hbm] * 5,
        out_specs=hbm,
        scratch_shapes=[
            pltpu.VMEM(blocks.shape, jnp.bfloat16),
            pltpu.VMEM(blocks.shape, jnp.bfloat16),
            pltpu.VMEM((2,) + blocks.shape, jnp.bfloat16),
            pltpu.VMEM((HALF, 8, 128), jnp.int32),
            pltpu.SMEM((HALF, 8, 128), jnp.int32),
            pltpu.VMEM(hidden_in.shape, jnp.bfloat16),
            pltpu.VMEM((rows, HQ, HD), jnp.float32),
            pltpu.VMEM((rows, HQ, HD), jnp.bfloat16),
            pltpu.VMEM((total, HQ, HD), jnp.bfloat16),
            pltpu.VMEM((total, HQ, HD), jnp.bfloat16),
            pltpu.VMEM(new_kv.shape, jnp.bfloat16),
            pltpu.VMEM((rows, 2, 2 * KVH, HD), jnp.float32),
            pltpu.VMEM((2, rows, 2, 2 * KVH, HD), jnp.float32),
            pltpu.VMEM((HQ, HD), jnp.float32),
            dma((5,)),
            dma((HALF,)), dma((HALF,)), dma((HALF,)), dma((2, HALF)),
            dma((total,)), dma((total,)), dma((total,)), dma((rows,)),
            dma((rows,)), dma, dma((2,)),
        ],
        compiler_params=pltpu.CompilerParams(
            collective_id=0, has_side_effects=True, vmem_limit_bytes=56 * 1024 * 1024
        ),
    )(meta, hidden_in, new_kv, norm_gain.reshape(HQ, HD), blocks)
    return out.reshape(1, rows, HQ * HD)


def solution(mesh):
    return jax.shard_map(
        per_device,
        mesh=mesh,
        in_specs=(
            P("replica", None),
            P("section", None),
            P("section", "replica", None, None, None),
            P("section", "replica", None, None, None, None),
            P("replica"),
            P("replica", None),
        ),
        out_specs=P("section", "replica", None),
        check_vma=False,
    )
```

time: 187 us -> 158 us (0.84)
  the two profiles are of different devices: /device:TPU:454 before, /device:TPU:487 now
where the time goes in v2:
time: 158 us
  Pallas kernels  154 us (97%)
  local copies, waits for them, and re-layouts  3.65 us (2%)
    pallas_call x1, Pallas kernels, per_device(): pl.pallas_call(functools.partial(kernel, sections, replicas, rows), out_s...  154 us

profile of v2, /device:TPU:487, one launch (start us, length us, event | category | flops | bytes accessed | tf_op | source)
XLA Modules:
  0.0 158.2 jit_solution(7395172914699377725)
XLA Ops:
  0.0 0.8 reshape.50
  0.8 0.2 convert_reduce_fusion
  1.0 0.1 select_reduce_fusion
  1.1 0.7 pad_bitcast_fusion
  1.8 0.6 pad.18.meta_ref
  2.4 154.2 %shard_map.64 = bf16[8,64,128]{2,1,0:T(8,128)(2,1)} custom-call(s32[8,128]{1,0:T(8,128)} %pad.18.meta_ref, bf16[8,8192]{1,0:T(8,128)(2,1)} %hidden_ref.1, bf16[1,8,2,4,128]{4,3,2,1,0:T(4,128)(2,1)} %new_ref.1, f32[64,128]{1,0:T(8,128)} %bitcast.10, bf16[16,2,4,128,128]{4,3,2,1,0:T(8,128)(2,1)} %bitcast.9), custom_call_target="tpu_custom_call" | custom-call | tf_op jit(solution)/shard_map/pallas_call | solution.py:313
  156.6 1.6 %reshape.52 = bf16[1,8,8192]{2,1,0:T(8,128)(2,1)} reshape(bf16[8,64,128]{2,1,0:T(8,128)(2,1)} %shard_map.64) | data formatting | bytes 262144 | tf_op jit(solution)/shard_map/reshape | solution.py:342
  (3 shorter events, 0.0 us)

commit v3 on v2

v3 whole, which is shorter than its diff:
```python
import functools
import math

import jax
import jax.numpy as jnp
from jax import lax
from jax.experimental import pallas as pl
from jax.experimental.pallas import tpu as pltpu
from jax.sharding import PartitionSpec as P

HQ = 64
KVH = 4
HD = 128
BLK = 128
NB = 2
GROUP = HQ // KVH
HALF = 8
MID = 4
PLANES = 4
MESH = pl.DeviceIdType.MESH


def dot_t(a, b):
    return lax.dot_general(a, b, (((1,), (1,)), ((), ())), preferred_element_type=jnp.float32)


def dot(a, b):
    return jnp.dot(a, b, preferred_element_type=jnp.float32)


def layer_row(x, gain, kv, slots, length, new):
    xf = x.astype(jnp.float32)
    q = (xf * gain).astype(jnp.bfloat16)
    square = jnp.sum(jnp.sum(xf * xf, axis=0, keepdims=True), axis=1, keepdims=True)
    factor = lax.rsqrt(square * (1.0 / (HQ * HD)) + 1e-05) * (math.log2(math.e) / HD**0.5)
    heads = [slice(h * GROUP, (h + 1) * GROUP) for h in range(KVH)]
    pad = jnp.zeros((BLK - 2 * KVH, HD), jnp.float32)
    new_keys, new_values = [
        jnp.concatenate([new[i], pad], axis=0).astype(jnp.bfloat16) for i in range(2)
    ]
    pos = lax.broadcasted_iota(jnp.int32, (1, BLK), 1)
    own = lax.broadcasted_iota(jnp.int32, (HQ, BLK), 0) // GROUP
    masks = [pos + j * BLK < length for j in range(NB)]
    masks.append(lax.broadcasted_iota(jnp.int32, (HQ, BLK), 1) == own)
    cached = jnp.concatenate(
        [
            dot(q[rows], jnp.concatenate([kv[slots[j], 0, h] for j in range(NB)], axis=1))
            for h, rows in enumerate(heads)
        ],
        axis=0,
    )
    scores = [cached[:, j * BLK : (j + 1) * BLK] for j in range(NB)]
    scores.append(dot_t(q, new_keys))
    scores = [part + jnp.where(mask, 0.0, -1e30) for part, mask in zip(scores, masks)]
    top = jnp.max(functools.reduce(jnp.maximum, scores), axis=1, keepdims=True)
    expos = [jnp.exp2((part - top) * factor) for part in scores]
    total = jnp.sum(sum(expos), axis=1, keepdims=True)
    weights = [part.astype(jnp.bfloat16) for part in expos]
    cached = jnp.concatenate(weights[:NB], axis=1)
    attended = dot(weights[NB], new_values) + jnp.concatenate(
        [
            dot(cached[rows], jnp.concatenate([kv[slots[j], 1, h] for j in range(NB)], axis=0))
            for h, rows in enumerate(heads)
        ],
        axis=0,
    )
    return (xf + attended / total).astype(jnp.bfloat16)


def kernel(
    sections, replicas, rows,
    meta_ref, hidden_ref, new_ref, gain_ref, parked_ref, out_ref,
    park, send, stage, kv_even, kv_odd, metav, metas, hidden, hidden_f, first, x_in, x_out,
    new_raw, new_own, new_in, gains,
    local_sem, meta_send, meta_recv, side_send, stage_recv, pass_send, own_send, kv_recv,
    x_send, x_recv, out_send, out_recv, first_send, new_send, new_recv, gain_send, gain_recv,
):
    s = lax.axis_index("section")
    p = lax.axis_index("replica")
    core = lax.rem(p, 2)
    chip = p // 2
    width = sections // PLANES
    plane = s // width
    worker = core == 1
    side = width * (1 - 2 * lax.rem(chip, 2))

    def at(shift):
        return lax.rem(p + shift + 2 * replicas, replicas)

    def sec(shift):
        return lax.rem(s + shift + 2 * sections, sections)

    def remote(src, dst, send_sem, recv_sem, section, replica):
        return pltpu.make_async_remote_copy(
            src, dst, send_sem, recv_sem,
            device_id={"section": section, "replica": replica}, device_id_type=MESH,
        )

    def local(i, src, dst):
        return pltpu.make_async_copy(src, dst, local_sem.at[i])

    fetch = [
        local(0, parked_ref, park),
        local(1, hidden_ref, hidden),
        local(2, new_ref, new_raw),
        local(3, gain_ref, gains.at[1]),
    ]
    for copy in fetch:
        copy.start()

    barrier = pltpu.get_barrier_semaphore()

    def greet(section, replica):
        pl.semaphore_signal(
            barrier, inc=1, device_id={"section": section, "replica": replica}, device_id_type=MESH
        )

    @pl.loop(1, replicas)
    def _(j):
        greet(s, at(j))

    greet(sec(width), p)
    greet(sec(-width), p)

    @pl.when(worker)
    def _():
        greet(sec(-side), at(-1))
        greet(sec(-side), at(MID - 1))
        greet(sec(-1), p)

    @pl.when(core == 0)
    def _():
        greet(sec(side), at(HALF + MID + 1))

    pl.semaphore_wait(barrier, replicas - 1 + 2 + 2)

    def meta_copy(k):
        return remote(
            meta_ref, metav.at[k], meta_send.at[k], meta_recv.at[k], s, at(HALF + k)
        )

    my_section = sec(side * (1 - core))
    mine = at(HALF + MID + 1 - core)

    def first_copy(m):
        return remote(
            first.at[m], x_in.at[core * rows + m], first_send.at[m], x_recv.at[core * rows + m],
            my_section, mine,
        )

    new_copy = remote(
        new_own, new_in.at[core], new_send, new_recv.at[core], my_section, mine
    )
    gain_copy = remote(gain_ref, gains.at[0], gain_send, gain_recv, sec(side), p)

    @pl.loop(0, HALF)
    def _(k):
        meta_copy(k).start()

    @pl.loop(0, HALF)
    def _(k):
        meta_copy(k).wait_recv()

    to_smem = local(4, metav, metas)
    to_smem.start()
    to_smem.wait()
    fetch[0].wait()

    def even(e):
        return 2 * e + core

    def odd(e):
        return 2 * e + 1 - core

    def target(k):
        to = p + MID - k + 2 * replicas
        return lax.rem(to - lax.rem(to, 2) + 1, replicas)

    def unit(k):
        return send.at[pl.ds(NB * k, NB)]

    def held(home, k):
        return (kv_even, kv_odd)[home].at[pl.ds(NB * k, NB)]

    def pick(k):
        for j in range(NB):
            block = metas[k, 0, NB * k + j]
            for h in range(KVH):
                send[NB * k + j, 0, h] = park[block, 0, h].T
                send[NB * k + j, 1, h] = park[block, 1, h]

    def side_copy(e):
        to = sec(side * (1 - 2 * lax.rem(e, 2)))
        return remote(unit(even(e)), stage.at[e], side_send.at[e], stage_recv.at[e], to, p)

    def near_copy(e=2):
        k = even(e)
        return remote(
            unit(k), held(0, k), side_send.at[e], kv_recv.at[0, k], sec(side), target(k)
        )

    def pass_copy(e):
        k = even(e)
        return remote(stage.at[e], held(0, k), pass_send.at[e], kv_recv.at[0, k], s, target(k))

    def own_copy(e):
        k = odd(e)
        return remote(unit(k), held(1, k), own_send.at[e], kv_recv.at[1, k], s, target(k))

    def own_stay(e):
        k = odd(e)
        return pltpu.make_async_copy(unit(k), held(1, k), kv_recv.at[1, k])

    def own_start_one(e):
        @pl.when(target(odd(e)) != p)
        def _():
            own_copy(e).start()

        @pl.when(target(odd(e)) == p)
        def _():
            own_stay(e).start()

    def own_start():
        @pl.loop(0, 4)
        def _(e):
            own_start_one(e)

    def own_wait():
        @pl.loop(0, 4)
        def _(e):
            @pl.when(target(odd(e)) != p)
            def _():
                own_copy(e).wait_send()

    def pass_start_one(e):
        side_copy(e).wait_recv()
        pass_copy(e).start()

    def from_plane(step, zero, one):
        @pl.when(side == -step * width)
        def _():
            zero(0)

        @pl.when(side == step * width)
        def _():
            one(1)
            one(3)

    def pass_start(step):
        from_plane(step, pass_start_one, pass_start_one)

    def pass_wait(step):
        def wait(e):
            pass_copy(e).wait_send()

        from_plane(step, wait, wait)

    @pl.loop(0, 2)
    def _(e):
        pick(even(e))
        side_copy(e).start()

    @pl.loop(0, 4)
    def _(e):
        pick(odd(e))

        @pl.when(plane == 0)
        def _():
            own_start_one(e)

    pick(even(3))
    pick(even(2))

    fetch[1].wait()
    fetch[2].wait()
    fetch[3].wait()

    @pl.loop(0, rows)
    def _(m):
        pair = new_raw[0, m].astype(jnp.float32)
        new_own[m, 0] = jnp.concatenate([pair[0], pair[1]], axis=0)
        new_own[m, 1] = jnp.concatenate([pair[1], pair[0]], axis=0)

    new_copy.start()

    @pl.when(worker)
    def _():
        gain_copy.start()

    @pl.when(s == 0)
    def _():
        for h in range(HQ):
            hidden_f[:, h, :] = hidden[:, h * HD : (h + 1) * HD].astype(jnp.float32)

        @pl.loop(0, rows)
        def _(m):
            first[m] = hidden_f[m].astype(jnp.bfloat16)
            first_copy(m).start()

    side_copy(0).wait_send()
    near_copy().start()
    side_copy(1).wait_send()
    side_copy(3).start()

    last_plane = PLANES - 1

    @pl.when(plane == 0)
    def _():
        own_wait()
        pass_start(1)

    @pl.when((plane > 0) & (plane < last_plane))
    def _():
        pass_start(-1)
        pass_wait(-1)
        own_start()

    @pl.when(plane == last_plane)
    def _():
        pass_start(1)
        pass_wait(1)
        pass_start(-1)

    def third():
        @pl.when(plane == 0)
        def _():
            pass_wait(1)
            pass_start(-1)
            pass_wait(-1)

        @pl.when((plane > 0) & (plane < last_plane))
        def _():
            own_wait()
            pass_start(1)
            pass_wait(1)

        @pl.when(plane == last_plane)
        def _():
            pass_wait(-1)
            own_start()
            own_wait()

    def relay_copy(i, section):
        return remote(x_out.at[i], x_in.at[i], x_send.at[i], x_recv.at[i], section, p)

    def home_copy(home, m, section, replica):
        return remote(
            x_out.at[home * rows + m], out_ref.at[m], out_send.at[home * rows + m], out_recv.at[m],
            section, replica,
        )

    def work(home):
        layer = sec(-side * (1 - home))
        remote(new_own, new_in.at[home], new_send, new_recv.at[home], s, p).wait_recv()

        if home == 0:
            gain_copy.wait_recv()

        @pl.loop(0, HALF)
        def _(k):
            remote(unit(k), held(home, k), own_send.at[0], kv_recv.at[home, k], s, p).wait_recv()

        @pl.loop(0, rows)
        def _(m):
            i = home * rows + m
            info = MID + 1 - home
            relay_copy(i, s).wait_recv()
            slots = [metas[info, 1, j * rows + m] for j in range(NB)]
            length = metas[info, 2, m]
            x_out[i] = layer_row(
                x_in[i], gains[home], (kv_even, kv_odd)[home], slots, length, new_in[home, m]
            )

            @pl.when(layer < sections - 1)
            def _():
                relay_copy(i, sec(1)).start()

            home_copy(home, m, layer, at(MID - 1 + home)).start()

    def work_wait(home):
        layer = sec(-side * (1 - home))

        @pl.loop(0, rows)
        def _(m):
            @pl.when(layer < sections - 1)
            def _():
                relay_copy(home * rows + m, sec(1)).wait_send()

            home_copy(home, m, layer, at(MID - 1 + home)).wait_send()

    other = sec(-side)
    early = jnp.minimum(s, other) < width
    odd_first = (other > s).astype(jnp.int32)
    third_turn = jnp.where(worker & early, 2 - odd_first, 0)

    @pl.loop(0, 3)
    def _(turn):
        @pl.when(turn == third_turn)
        def _():
            third()

        @pl.when(worker & (turn == 1))
        def _():
            work(0)

        @pl.when(worker & (turn == 2 - 2 * odd_first))
        def _():
            work(1)

    @pl.when(worker)
    def _():
        work_wait(0)
        work_wait(1)
        gain_copy.wait_send()

    @pl.loop(0, HALF)
    def _(k):
        meta_copy(k).wait_send()

    near_copy().wait_send()
    side_copy(3).wait_send()
    new_copy.wait_send()

    @pl.loop(0, rows)
    def _(m):
        @pl.when(s == 0)
        def _():
            first_copy(m).wait_send()

        home_copy(0, m, s, p).wait_recv()


def per_device(hidden_in, norm_gain, new_kv, parked, cache_len, block_home):
    replicas = lax.axis_size("replica")
    sections = lax.axis_size("section")
    me = lax.axis_index("replica")
    blocks = parked[0]
    park_count = blocks.shape[0]
    rows = block_home.shape[0]
    count = rows * NB

    flat = block_home.T.reshape(count)
    near = lax.rem(flat - (me + HALF) * park_count + 2 * replicas * park_count, replicas * park_count)
    place = jnp.sum((near[None, :] < near[:, None]).astype(jnp.int32), axis=1)
    hit = place[None, :] == jnp.arange(count, dtype=jnp.int32)[:, None]
    local = jnp.sum(jnp.where(hit, lax.rem(flat, park_count)[None, :], 0), axis=1)
    meta = jnp.stack([
        jnp.pad(local, (0, 128 - count)),
        jnp.pad(place, (0, 128 - count)),
        jnp.pad(cache_len, (0, 128 - rows)),
    ])
    meta = jnp.pad(meta, ((0, 5), (0, 0)))

    total = 2 * rows
    hbm = pl.BlockSpec(memory_space=pl.ANY)
    dma = pltpu.SemaphoreType.DMA
    out = pl.pallas_call(
        functools.partial(kernel, sections, replicas, rows),
        out_shape=jax.ShapeDtypeStruct((rows, HQ, HD), jnp.bfloat16),
        in_specs=[hbm] * 5,
        out_specs=hbm,
        scratch_shapes=[
            pltpu.VMEM(blocks.shape, jnp.bfloat16),
            pltpu.VMEM(blocks.shape, jnp.bfloat16),
            pltpu.VMEM((4, NB) + blocks.shape[1:], jnp.bfloat16),
            pltpu.VMEM(blocks.shape, jnp.bfloat16),
            pltpu.VMEM(blocks.shape, jnp.bfloat16),
            pltpu.VMEM((HALF, 8, 128), jnp.int32),
            pltpu.SMEM((HALF, 8, 128), jnp.int32),
            pltpu.VMEM(hidden_in.shape, jnp.bfloat16),
            pltpu.VMEM((rows, HQ, HD), jnp.float32),
            pltpu.VMEM((rows, HQ, HD), jnp.bfloat16),
            pltpu.VMEM((total, HQ, HD), jnp.bfloat16),
            pltpu.VMEM((total, HQ, HD), jnp.bfloat16),
            pltpu.VMEM(new_kv.shape, jnp.bfloat16),
            pltpu.VMEM((rows, 2, 2 * KVH, HD), jnp.float32),
            pltpu.VMEM((2, rows, 2, 2 * KVH, HD), jnp.float32),
            pltpu.VMEM((2, HQ, HD), jnp.float32),
            dma((5,)),
            dma((HALF,)), dma((HALF,)), dma((4,)), dma((4,)), dma((4,)), dma((4,)), dma((2, HALF)),
            dma((total,)), dma((total,)), dma((total,)), dma((rows,)),
            dma((rows,)), dma, dma((2,)), dma, dma,
        ],
        compiler_params=pltpu.CompilerParams(
            collective_id=0, has_side_effects=True, vmem_limit_bytes=56 * 1024 * 1024
        ),
    )(meta, hidden_in, new_kv, norm_gain.reshape(HQ, HD), blocks)
    return out.reshape(1, rows, HQ * HD)


def solution(mesh):
    return jax.shard_map(
        per_device,
        mesh=mesh,
        in_specs=(
            P("replica", None),
            P("section", None),
            P("section", "replica", None, None, None),
            P("section", "replica", None, None, None, None),
            P("replica"),
            P("replica", None),
        ),
        out_specs=P("section", "replica", None),
        check_vma=False,
    )
```

time: 158 us -> 145 us (0.918)
  the two profiles are of different devices: /device:TPU:487 before, /device:TPU:463 now
where the time goes in v3:
time: 145 us
  Pallas kernels  141 us (97%)
  local copies, waits for them, and re-layouts  3.65 us (3%)
    pallas_call x1, Pallas kernels, per_device(): pl.pallas_call(functools.partial(kernel, sections, replicas, rows), out_s...  141 us

profile of v3, /device:TPU:463, one launch (start us, length us, event | category | flops | bytes accessed | tf_op | source)
XLA Modules:
  0.0 145.2 jit_solution(11947443426488455780)
XLA Ops:
  0.0 0.8 reshape.50
  0.8 0.2 convert_reduce_fusion
  1.0 0.1 select_reduce_fusion
  1.1 0.7 pad_bitcast_fusion
  1.8 0.6 pad.18.meta_ref
  2.4 141.3 %shard_map.64 = bf16[8,64,128]{2,1,0:T(8,128)(2,1)} custom-call(s32[8,128]{1,0:T(8,128)} %pad.18.meta_ref, bf16[8,8192]{1,0:T(8,128)(2,1)} %hidden_ref.1, bf16[1,8,2,4,128]{4,3,2,1,0:T(4,128)(2,1)} %new_ref.1, f32[64,128]{1,0:T(8,128)} %bitcast.10, bf16[16,2,4,128,128]{4,3,2,1,0:T(8,128)(2,1)} %bitcast.9), custom_call_target="tpu_custom_call" | custom-call | tf_op jit(solution)/shard_map/pallas_call | solution.py:457
  143.6 1.6 %reshape.52 = bf16[1,8,8192]{2,1,0:T(8,128)(2,1)} reshape(bf16[8,64,128]{2,1,0:T(8,128)(2,1)} %shard_map.64) | data formatting | bytes 262144 | tf_op jit(solution)/shard_map/reshape | solution.py:488
  (3 shorter events, 0.0 us)

commit v4 on v3

--- a/solution.py
+++ b/solution.py
@@ -69,10 +69,10 @@
 
 def kernel(
     sections, replicas, rows,
-    meta_ref, hidden_ref, new_ref, gain_ref, parked_ref, out_ref,
-    park, send, stage, kv_even, kv_odd, metav, metas, hidden, hidden_f, first, x_in, x_out,
+    table_ref, length_ref, hidden_ref, new_ref, gain_ref, parked_ref, out_ref,
+    park, send, stage, kv_even, kv_odd, table, lengths, meta, metav, metas, hidden, hidden_f, first, x_in, x_out,
     new_raw, new_own, new_in, gains,
-    local_sem, meta_send, meta_recv, side_send, stage_recv, pass_send, own_send, kv_recv,
+    local_sem, meta_send, meta_recv, side_send, stage_recv, pass_send, own_send, even_recv, odd_recv,
     x_send, x_recv, out_send, out_recv, first_send, new_send, new_recv, gain_send, gain_recv,
 ):
     s = lax.axis_index("section")
@@ -104,6 +104,8 @@
         local(1, hidden_ref, hidden),
         local(2, new_ref, new_raw),
         local(3, gain_ref, gains.at[1]),
+        local(4, table_ref, table),
+        local(5, length_ref, lengths),
     ]
     for copy in fetch:
         copy.start()
@@ -132,11 +134,37 @@
     def _():
         greet(sec(side), at(HALF + MID + 1))
 
+    count = NB * rows
+    parks = park.shape[0]
+    fetch[4].wait()
+    fetch[5].wait()
+    blocks = [table[j, m] for j in range(NB) for m in range(rows)]
+    near = [
+        lax.rem(b - (p + HALF) * parks + 2 * replicas * parks, replicas * parks) for b in blocks
+    ]
+    row = lax.broadcasted_iota(jnp.int32, meta.shape, 0)
+    lane = lax.broadcasted_iota(jnp.int32, meta.shape, 1)
+    info = jnp.zeros(meta.shape, jnp.int32)
+    for e in range(count):
+        place = sum((near[i] < near[e]).astype(jnp.int32) for i in range(count) if i != e)
+        info = jnp.where((row == 0) & (lane == place), lax.rem(blocks[e], parks), info)
+        info = jnp.where((row == 1) & (lane == e), place, info)
+    for m in range(rows):
+        info = jnp.where((row == 2) & (lane == m), lengths[0, m], info)
+    meta[...] = info
+
+    def turn_keys(b):
+        for h in range(KVH):
+            park[b, 0, h] = park[b, 0, h].T
+
+    fetch[0].wait()
+    pl.loop(0, parks // 2)(turn_keys)
+
     pl.semaphore_wait(barrier, replicas - 1 + 2 + 2)
 
     def meta_copy(k):
         return remote(
-            meta_ref, metav.at[k], meta_send.at[k], meta_recv.at[k], s, at(HALF + k)
+            meta, metav.at[k], meta_send.at[k], meta_recv.at[k], s, at(HALF + k)
         )
 
     my_section = sec(side * (1 - core))
@@ -157,14 +185,17 @@
     def _(k):
         meta_copy(k).start()
 
-    @pl.loop(0, HALF)
-    def _(k):
-        meta_copy(k).wait_recv()
-
-    to_smem = local(4, metav, metas)
-    to_smem.start()
-    to_smem.wait()
-    fetch[0].wait()
+    pl.loop(parks // 2, parks)(turn_keys)
+
+    def meta_wait(first, last):
+        @pl.loop(first, last)
+        def _(k):
+            meta_copy(k).wait_recv()
+
+        some = pl.ds(first, last - first)
+        to_smem = local(6, metav.at[some], metas.at[some])
+        to_smem.start()
+        to_smem.wait()
 
     def even(e):
         return 2 * e + core
@@ -186,30 +217,36 @@
         for j in range(NB):
             block = metas[k, 0, NB * k + j]
             for h in range(KVH):
-                send[NB * k + j, 0, h] = park[block, 0, h].T
+                send[NB * k + j, 0, h] = park[block, 0, h]
                 send[NB * k + j, 1, h] = park[block, 1, h]
 
-    def side_copy(e):
+    def piece(k, j):
+        return send.at[pl.ds(NB * k + j, 1)], kv_even.at[pl.ds(NB * k + j, 1)], even_recv.at[k, j]
+
+    def side_copy(e, j):
         to = sec(side * (1 - 2 * lax.rem(e, 2)))
-        return remote(unit(even(e)), stage.at[e], side_send.at[e], stage_recv.at[e], to, p)
-
-    def near_copy(e=2):
-        k = even(e)
+        src, _, _ = piece(even(e), j)
         return remote(
-            unit(k), held(0, k), side_send.at[e], kv_recv.at[0, k], sec(side), target(k)
-        )
-
-    def pass_copy(e):
-        k = even(e)
-        return remote(stage.at[e], held(0, k), pass_send.at[e], kv_recv.at[0, k], s, target(k))
+            src, stage.at[e, pl.ds(j, 1)], side_send.at[e, j], stage_recv.at[e, j], to, p
+        )
+
+    def near_copy(j, e=2):
+        src, dst, sem = piece(even(e), j)
+        return remote(src, dst, side_send.at[e, j], sem, sec(side), target(even(e)))
+
+    def pass_copy(e, j):
+        _, dst, sem = piece(even(e), j)
+        return remote(
+            stage.at[e, pl.ds(j, 1)], dst, pass_send.at[e, j], sem, s, target(even(e))
+        )
 
     def own_copy(e):
         k = odd(e)
-        return remote(unit(k), held(1, k), own_send.at[e], kv_recv.at[1, k], s, target(k))
+        return remote(unit(k), held(1, k), own_send.at[e], odd_recv.at[k], s, target(k))
 
     def own_stay(e):
         k = odd(e)
-        return pltpu.make_async_copy(unit(k), held(1, k), kv_recv.at[1, k])
+        return pltpu.make_async_copy(unit(k), held(1, k), odd_recv.at[k])
 
     def own_start_one(e):
         @pl.when(target(odd(e)) != p)
@@ -219,11 +256,6 @@
         @pl.when(target(odd(e)) == p)
         def _():
             own_stay(e).start()
-
-    def own_start():
-        @pl.loop(0, 4)
-        def _(e):
-            own_start_one(e)
 
     def own_wait():
         @pl.loop(0, 4)
@@ -233,8 +265,9 @@
                 own_copy(e).wait_send()
 
     def pass_start_one(e):
-        side_copy(e).wait_recv()
-        pass_copy(e).start()
+        for j in range(NB):
+            side_copy(e, j).wait_recv()
+            pass_copy(e, j).start()
 
     def from_plane(step, zero, one):
         @pl.when(side == -step * width)
@@ -243,32 +276,43 @@
 
         @pl.when(side == step * width)
         def _():
+            one(3)
             one(1)
-            one(3)
 
     def pass_start(step):
         from_plane(step, pass_start_one, pass_start_one)
 
     def pass_wait(step):
         def wait(e):
-            pass_copy(e).wait_send()
+            for j in range(NB):
+                pass_copy(e, j).wait_send()
 
         from_plane(step, wait, wait)
 
-    @pl.loop(0, 2)
-    def _(e):
-        pick(even(e))
-        side_copy(e).start()
+    waits = lax.rem(plane, 2) == 1
+
+    def goes_first(e):
+        return jnp.logical_not(waits) | (e == 3 * (1 - core))
+
+    meta_wait(HALF - 2, HALF)
+    pick(even(3))
+    for j in range(NB):
+        side_copy(3, j).start()
+
+    meta_wait(0, HALF - 2)
+    pick(even(0))
+    for j in range(NB):
+        side_copy(0, j).start()
 
     @pl.loop(0, 4)
     def _(e):
         pick(odd(e))
 
-        @pl.when(plane == 0)
+        @pl.when(goes_first(e))
         def _():
             own_start_one(e)
 
-    pick(even(3))
+    pick(even(1))
     pick(even(2))
 
     fetch[1].wait()
@@ -297,48 +341,36 @@
             first[m] = hidden_f[m].astype(jnp.bfloat16)
             first_copy(m).start()
 
-    side_copy(0).wait_send()
-    near_copy().start()
-    side_copy(1).wait_send()
-    side_copy(3).start()
-
-    last_plane = PLANES - 1
+    for j in range(NB):
+        side_copy(3, j).wait_send()
+        side_copy(1, j).start()
+        side_copy(0, j).wait_send()
+        near_copy(j).start()
+
+    lead = jnp.where((plane == 0) | (plane == PLANES - 1), 1, -1)
 
     @pl.when(plane == 0)
     def _():
         own_wait()
-        pass_start(1)
-
-    @pl.when((plane > 0) & (plane < last_plane))
-    def _():
-        pass_start(-1)
-        pass_wait(-1)
-        own_start()
-
-    @pl.when(plane == last_plane)
-    def _():
-        pass_start(1)
-        pass_wait(1)
-        pass_start(-1)
-
-    def third():
-        @pl.when(plane == 0)
-        def _():
-            pass_wait(1)
-            pass_start(-1)
-            pass_wait(-1)
-
-        @pl.when((plane > 0) & (plane < last_plane))
-        def _():
-            own_wait()
-            pass_start(1)
-            pass_wait(1)
-
-        @pl.when(plane == last_plane)
-        def _():
-            pass_wait(-1)
-            own_start()
-            own_wait()
+
+    pass_start(lead)
+
+    @pl.when(waits)
+    def _():
+        pass_wait(lead)
+
+        @pl.loop(0, 4)
+        def _(e):
+            @pl.when(jnp.logical_not(goes_first(e)))
+            def _():
+                own_start_one(e)
+
+    def passes_left():
+        @pl.when(jnp.logical_not(waits))
+        def _():
+            pass_wait(lead)
+
+        pass_start(-lead)
 
     def relay_copy(i, section):
         return remote(x_out.at[i], x_in.at[i], x_send.at[i], x_recv.at[i], section, p)
@@ -358,7 +390,12 @@
 
         @pl.loop(0, HALF)
         def _(k):
-            remote(unit(k), held(home, k), own_send.at[0], kv_recv.at[home, k], s, p).wait_recv()
+            if home == 0:
+                for j in range(NB):
+                    src, dst, sem = piece(k, j)
+                    remote(src, dst, side_send.at[0, j], sem, s, p).wait_recv()
+            else:
+                remote(unit(k), held(1, k), own_send.at[0], odd_recv.at[k], s, p).wait_recv()
 
         @pl.loop(0, rows)
         def _(m):
@@ -391,13 +428,13 @@
     other = sec(-side)
     early = jnp.minimum(s, other) < width
     odd_first = (other > s).astype(jnp.int32)
-    third_turn = jnp.where(worker & early, 2 - odd_first, 0)
+    left_turn = jnp.where(worker & early, 2 - odd_first, 0)
 
     @pl.loop(0, 3)
     def _(turn):
-        @pl.when(turn == third_turn)
-        def _():
-            third()
+        @pl.when(turn == left_turn)
+        def _():
+            passes_left()
 
         @pl.when(worker & (turn == 1))
         def _():
@@ -417,8 +454,16 @@
     def _(k):
         meta_copy(k).wait_send()
 
-    near_copy().wait_send()
-    side_copy(3).wait_send()
+    for j in range(NB):
+        near_copy(j).wait_send()
+        side_copy(1, j).wait_send()
+
+    pass_wait(-lead)
+
+    @pl.when(plane > 0)
+    def _():
+        own_wait()
+
     new_copy.wait_send()
 
     @pl.loop(0, rows)
@@ -433,31 +478,15 @@
 def per_device(hidden_in, norm_gain, new_kv, parked, cache_len, block_home):
     replicas = lax.axis_size("replica")
     sections = lax.axis_size("section")
-    me = lax.axis_index("replica")
     blocks = parked[0]
-    park_count = blocks.shape[0]
     rows = block_home.shape[0]
-    count = rows * NB
-
-    flat = block_home.T.reshape(count)
-    near = lax.rem(flat - (me + HALF) * park_count + 2 * replicas * park_count, replicas * park_count)
-    place = jnp.sum((near[None, :] < near[:, None]).astype(jnp.int32), axis=1)
-    hit = place[None, :] == jnp.arange(count, dtype=jnp.int32)[:, None]
-    local = jnp.sum(jnp.where(hit, lax.rem(flat, park_count)[None, :], 0), axis=1)
-    meta = jnp.stack([
-        jnp.pad(local, (0, 128 - count)),
-        jnp.pad(place, (0, 128 - count)),
-        jnp.pad(cache_len, (0, 128 - rows)),
-    ])
-    meta = jnp.pad(meta, ((0, 5), (0, 0)))
-
     total = 2 * rows
     hbm = pl.BlockSpec(memory_space=pl.ANY)
     dma = pltpu.SemaphoreType.DMA
     out = pl.pallas_call(
         functools.partial(kernel, sections, replicas, rows),
         out_shape=jax.ShapeDtypeStruct((rows, HQ, HD), jnp.bfloat16),
-        in_specs=[hbm] * 5,
+        in_specs=[hbm] * 6,
         out_specs=hbm,
         scratch_shapes=[
             pltpu.VMEM(blocks.shape, jnp.bfloat16),
@@ -465,6 +494,9 @@
             pltpu.VMEM((4, NB) + blocks.shape[1:], jnp.bfloat16),
             pltpu.VMEM(blocks.shape, jnp.bfloat16),
             pltpu.VMEM(blocks.shape, jnp.bfloat16),
+            pltpu.SMEM((NB, rows), jnp.int32),
+            pltpu.SMEM((1, rows), jnp.int32),
+            pltpu.VMEM((8, 128), jnp.int32),
             pltpu.VMEM((HALF, 8, 128), jnp.int32),
             pltpu.SMEM((HALF, 8, 128), jnp.int32),
             pltpu.VMEM(hidden_in.shape, jnp.bfloat16),
@@ -476,15 +508,16 @@
             pltpu.VMEM((rows, 2, 2 * KVH, HD), jnp.float32),
             pltpu.VMEM((2, rows, 2, 2 * KVH, HD), jnp.float32),
             pltpu.VMEM((2, HQ, HD), jnp.float32),
-            dma((5,)),
-            dma((HALF,)), dma((HALF,)), dma((4,)), dma((4,)), dma((4,)), dma((4,)), dma((2, HALF)),
+            dma((7,)),
+            dma((HALF,)), dma((HALF,)), dma((4, NB)), dma((4, NB)), dma((4, NB)), dma((4,)),
+            dma((HALF, NB)), dma((HALF,)),
             dma((total,)), dma((total,)), dma((total,)), dma((rows,)),
             dma((rows,)), dma, dma((2,)), dma, dma,
         ],
         compiler_params=pltpu.CompilerParams(
             collective_id=0, has_side_effects=True, vmem_limit_bytes=56 * 1024 * 1024
         ),
-    )(meta, hidden_in, new_kv, norm_gain.reshape(HQ, HD), blocks)
+    )(block_home.T, cache_len.reshape(1, rows), hidden_in, new_kv, norm_gain.reshape(HQ, HD), blocks)
     return out.reshape(1, rows, HQ * HD)
 
 

time: 145 us -> 129 us (0.89)
  the two profiles are of different devices: /device:TPU:463 before, /device:TPU:454 now
where the time goes in v4:
time: 129 us
  Pallas kernels  127 us (98%)
  local copies, waits for them, and re-layouts  1.62 us (1%)
    pallas_call x1, Pallas kernels, per_device(): pl.pallas_call(functools.partial(kernel, sections, replicas, rows), out_s...  127 us

profile of v4, /device:TPU:454, one launch (start us, length us, event | category | flops | bytes accessed | tf_op | source)
XLA Modules:
  0.0 128.8 jit_solution(1826847538943267769)
XLA Ops:
  0.0 127.2 %shard_map.64 = bf16[8,64,128]{2,1,0:T(8,128)(2,1)} custom-call(s32[2,8]{1,0:T(2,128)} %bitcast.6, s32[1,8]{1,0:T(1,128)} %bitcast.7, bf16[8,8192]{1,0:T(8,128)(2,1)} %hidden_ref.1, bf16[1,8,2,4,128]{4,3,2,1,0:T(4,128)(2,1)} %new_ref.1, f32[64,128]{1,0:T(8,128)} %bitcast.5, bf16[16,2,4,128,128]{4,3,2,1,0:T(8,128)(2,1)} %bitcast.4), custom_call_target="tpu_custom_call" | custom-call | tf_op jit(solution)/shard_map/pallas_call | solution.py:486
  127.2 1.6 %reshape.11 = bf16[1,8,8192]{2,1,0:T(8,128)(2,1)} reshape(bf16[8,64,128]{2,1,0:T(8,128)(2,1)} %shard_map.64) | data formatting | bytes 262144 | tf_op jit(solution)/shard_map/reshape | solution.py:521

commit v5 on v4

--- a/solution.py
+++ b/solution.py
@@ -82,7 +82,7 @@
     width = sections // PLANES
     plane = s // width
     worker = core == 1
-    side = width * (1 - 2 * lax.rem(chip, 2))
+    side = width * (2 * lax.rem(chip, 2) - 1)
 
     def at(shift):
         return lax.rem(p + shift + 2 * replicas, replicas)
@@ -397,22 +397,40 @@
             else:
                 remote(unit(k), held(1, k), own_send.at[0], odd_recv.at[k], s, p).wait_recv()
 
-        @pl.loop(0, rows)
-        def _(m):
+        def row(m):
             i = home * rows + m
             info = MID + 1 - home
-            relay_copy(i, s).wait_recv()
             slots = [metas[info, 1, j * rows + m] for j in range(NB)]
-            length = metas[info, 2, m]
-            x_out[i] = layer_row(
-                x_in[i], gains[home], (kv_even, kv_odd)[home], slots, length, new_in[home, m]
+            return layer_row(
+                x_in[i], gains[home], (kv_even, kv_odd)[home], slots, metas[info, 2, m],
+                new_in[home, m],
             )
 
-            @pl.when(layer < sections - 1)
-            def _():
-                relay_copy(i, sec(1)).start()
-
-            home_copy(home, m, layer, at(MID - 1 + home)).start()
+        def step(ms):
+            for m in ms:
+                relay_copy(home * rows + m, s).wait_recv()
+            results = [row(m) for m in ms]
+            for m, result in zip(ms, results):
+                i = home * rows + m
+                x_out[i] = result
+
+                @pl.when(layer < sections - 1)
+                def _():
+                    relay_copy(i, sec(1)).start()
+
+                home_copy(home, m, layer, at(MID - 1 + home)).start()
+
+        @pl.when(layer == 0)
+        def _():
+            @pl.loop(0, rows // 2)
+            def _(t):
+                step([2 * t, 2 * t + 1])
+
+        @pl.when(layer > 0)
+        def _():
+            @pl.loop(0, rows)
+            def _(m):
+                step([m])
 
     def work_wait(home):
         layer = sec(-side * (1 - home))

time: 129 us -> 128 us (level)
  no operation moved by 1% of the time
where the time goes in v5:
time: 128 us
  Pallas kernels  127 us (99%)
  local copies, waits for them, and re-layouts  1.62 us (1%)
    pallas_call x1, Pallas kernels, per_device(): pl.pallas_call(functools.partial(kernel, sections, replicas, rows), out_s...  127 us

profile of v5, /device:TPU:454, one launch (start us, length us, event | category | flops | bytes accessed | tf_op | source)
XLA Modules:
  0.0 128.3 jit_solution(10174606326774431964)
XLA Ops:
  0.0 126.7 %shard_map.64 = bf16[8,64,128]{2,1,0:T(8,128)(2,1)} custom-call(s32[2,8]{1,0:T(2,128)} %bitcast.6, s32[1,8]{1,0:T(1,128)} %bitcast.7, bf16[8,8192]{1,0:T(8,128)(2,1)} %hidden_ref.1, bf16[1,8,2,4,128]{4,3,2,1,0:T(4,128)(2,1)} %new_ref.1, f32[64,128]{1,0:T(8,128)} %bitcast.5, bf16[16,2,4,128,128]{4,3,2,1,0:T(8,128)(2,1)} %bitcast.4), custom_call_target="tpu_custom_call" | custom-call | tf_op jit(solution)/shard_map/pallas_call | solution.py:504
  126.7 1.6 %reshape.11 = bf16[1,8,8192]{2,1,0:T(8,128)(2,1)} reshape(bf16[8,64,128]{2,1,0:T(8,128)(2,1)} %shard_map.64) | data formatting | bytes 262144 | tf_op jit(solution)/shard_map/reshape | solution.py:539
